TPU v7x, 256 devices: a whole 4x4x8 slice. The times are simulated.
256 devices in a mesh: img: 16 (over x, y), proto: 16 (over z, core).
Axes of the slice: x: 4, y: 4, z: 8, core: 2. Of those that a mesh axis runs over, the one named last changes fastest.
Arguments:
- student_patch_tokens: bfloat16 [16, 256, 4096], P('img', None, 'proto'), may hold values from -6 to 6
- teacher_patch_tokens: bfloat16 [16, 256, 4096], P('img', None, 'proto'), may hold values from -6 to 6
- mask_counts: int32 [16], P('img'), may hold values from 32 to 128, as said below
- mask_index: int32 [16, 128], P('img'), may hold values from 0 to 255, as said below
- student_bottleneck: bfloat16 [4096, 256], P('proto'), may hold values from -0.09375 to 0.09375
- teacher_bottleneck: bfloat16 [4096, 256], P('proto'), may hold values from -0.09375 to 0.09375
- student_protos: bfloat16 [256, 98304], P(None, 'proto'), may hold values from -60 to 60
- teacher_protos: bfloat16 [256, 98304], P(None, 'proto'), may hold values from -60 to 60
- center: float32 [98304], P('proto'), may hold values from -0.75 to 0.75
Outputs:
- image_loss: float32 [16], P('img')
- grad_protos: float32 [256, 98304], P('img', 'proto')
- grad_bottleneck: float32 [4096, 256], P('proto', 'img')
Inputs may be any that keep to these rules, and one draw needn't show every extreme that they name: `mask_counts`: some image has exactly 128 masked patches. `mask_index`: the 128 entries of an image are distinct patch numbers; only the first mask_counts of them are used.
All inputs are finite; a program needn't handle non-finite values.
Results may differ from a plain program's by a relative error of at most 0.0071.
Values may be sent and summed in bfloat16 or wider, within the bound.
A program may use at most 64 MiB of HBM per device.

v0:
```python
import jax
import jax.numpy as jnp
from jax import lax
from jax.sharding import PartitionSpec as P

EPSILON = 1e-06
STUDENT_TEMP = 0.1
TEACHER_TEMP = 0.04
LOSS_SCALE = 4096.0


def scores(units_student, units_teacher, weight, student_protos, teacher_protos, center):
    logits_student = (
        jnp.dot(units_student, student_protos, preferred_element_type=jnp.float32) / STUDENT_TEMP
    )
    logits_teacher = (
        jnp.dot(units_teacher, teacher_protos, preferred_element_type=jnp.float32) - center[None, :]
    ) / TEACHER_TEMP
    top_student, top_teacher = lax.pmax(
        (jnp.max(logits_student, axis=1), jnp.max(logits_teacher, axis=1)), "proto"
    )
    exp_student = jnp.exp(logits_student - top_student[:, None])
    exp_teacher = jnp.exp(logits_teacher - top_teacher[:, None])
    total_student, total_teacher, cross = lax.psum(
        (
            jnp.sum(exp_student, axis=1),
            jnp.sum(exp_teacher, axis=1),
            jnp.sum(exp_teacher * logits_student, axis=1),
        ),
        "proto",
    )
    loss_rows = -(cross / total_teacher - top_student - jnp.log(total_student))
    differ = exp_student / total_student[:, None] - exp_teacher / total_teacher[:, None]
    logit_gradient = (
        LOSS_SCALE * weight.astype(jnp.float32)[:, None] * differ / STUDENT_TEMP
    ).astype(jnp.bfloat16)
    return (loss_rows, logit_gradient)


def prototype_gradient(row_units, logit_gradient):
    return lax.psum_scatter(
        lax.dot_general(
            row_units, logit_gradient, (((0,), (0,)), ((), ())), preferred_element_type=jnp.float32
        ),
        "img",
        scatter_dimension=0,
        tiled=True,
    )


def per_device(
    student_patch_tokens,
    teacher_patch_tokens,
    mask_counts,
    mask_index,
    student_bottleneck,
    teacher_bottleneck,
    student_protos,
    teacher_protos,
    center,
):
    img_local, patch_total, width_local = student_patch_tokens.shape
    mask_width = mask_index.shape[1]
    rows_local = img_local * mask_width
    patch_iota = lax.broadcasted_iota(jnp.int32, (img_local, mask_width, patch_total), 2)
    masked_picker = (mask_index[:, :, None] == patch_iota).astype(jnp.bfloat16)
    student_token_rows = (
        jnp.einsum(
            "oaz,oze->oae", masked_picker, student_patch_tokens, preferred_element_type=jnp.float32
        )
        .astype(jnp.bfloat16)
        .reshape(rows_local, width_local)
    )
    teacher_rows = (
        jnp.einsum(
            "oaz,oze->oae", masked_picker, teacher_patch_tokens, preferred_element_type=jnp.float32
        )
        .astype(jnp.bfloat16)
        .reshape(rows_local, width_local)
    )
    partial_student = jnp.dot(
        student_token_rows, student_bottleneck, preferred_element_type=jnp.float32
    )
    partial_teacher = jnp.dot(teacher_rows, teacher_bottleneck, preferred_element_type=jnp.float32)
    hidden_student, hidden_teacher = lax.psum((partial_student, partial_teacher), "proto")
    inv_student = lax.rsqrt(
        jnp.sum(hidden_student * hidden_student, axis=1, keepdims=True) + EPSILON
    )
    inv_teacher = lax.rsqrt(
        jnp.sum(hidden_teacher * hidden_teacher, axis=1, keepdims=True) + EPSILON
    )
    units_student = (hidden_student * inv_student).astype(jnp.bfloat16)
    units_teacher = (hidden_teacher * inv_teacher).astype(jnp.bfloat16)
    position = lax.broadcasted_iota(jnp.int32, (img_local, mask_width), 1)
    live_grid = position < mask_counts[:, None]
    weight = (
        jnp.where(live_grid, 1.0 / mask_counts.astype(jnp.float32)[:, None], 0.0)
        .astype(jnp.bfloat16)
        .reshape(rows_local)
    )
    loss_rows, logit_gradient = scores(
        units_student, units_teacher, weight, student_protos, teacher_protos, center
    )
    weighted = weight.astype(jnp.float32) * loss_rows
    image_loss = jnp.sum(weighted.reshape(img_local, mask_width), axis=1)
    grad_protos = prototype_gradient(units_student, logit_gradient)
    partial_rows = lax.dot_general(
        logit_gradient, student_protos, (((1,), (1,)), ((), ())), preferred_element_type=jnp.float32
    )
    grad_rows = lax.psum(partial_rows, "proto")
    inner = jnp.sum(hidden_student * grad_rows, axis=1, keepdims=True)
    grad_hidden = (
        grad_rows * inv_student - hidden_student * inner * (inv_student * inv_student * inv_student)
    ).astype(jnp.bfloat16)
    local_term = lax.dot_general(
        student_token_rows,
        grad_hidden,
        (((0,), (0,)), ((), ())),
        preferred_element_type=jnp.float32,
    )
    grad_bottleneck = lax.psum_scatter(local_term, "img", scatter_dimension=1, tiled=True)
    return (image_loss, grad_protos, grad_bottleneck)


def solution(mesh):
    placed = (
        P("img", None, "proto"),
        P("img", None, "proto"),
        P("img"),
        P("img", None),
        P("proto", None),
        P("proto", None),
        P(None, "proto"),
        P(None, "proto"),
        P("proto"),
    )
    return jax.shard_map(
        per_device,
        mesh=mesh,
        in_specs=placed,
        out_specs=(P("img"), P("img", "proto"), P("proto", "img")),
        check_vma=False,
    )
```

profile of v0, /device:TPU:1, one launch (start us, length us, event | category | flops | bytes accessed | tf_op | source)
XLA Modules:
  0.0 476.9 jit_solution(15293048073121810471)
XLA Ops:
  7.2 0.0 copy-start
  7.2 0.0 all-reduce.8.cloned.1.call-start
  7.2 1.3 convolution_convert_fusion
  8.5 1.7 fusion.25
  10.2 2.0 fusion.3
  12.2 0.0 all-reduce.8.cloned.1.call-update
  12.2 0.0 all-reduce.6.cloned.1.call-start
  13.0 112.1 %all-reduce.8.cloned.1.call-done = (f32[128,256]{1,0:T(8,128)}, f32[128,256]{1,0:T(8,128)}) async-done(((f32[128,256]{1,0:T(8,128)}, f32[128,256]{1,0:T(8,128)}), (f32[128,256]{1,0:T(8,128)}, f32[128,256]{1,0:T(8,128)})) %all-reduce.8.cloned.1.call-update) | async-done | bytes 262160 | tf_op jit(solution)/shard_map/psum | solution.py:85
  125.0 1.1 multiply_reduce_fusion.2
  126.1 0.0 copy-done
  126.1 0.0 copy-start.3
  126.2 0.0 copy-start.4
  126.2 0.0 copy-start.5
  126.2 3.4 fusion.24
  129.6 0.0 copy-done.3
  129.6 0.0 copy-done.4
  129.6 0.0 copy-done.5
  129.6 2.4 fusion.23
  132.0 23.5 %all-reduce.2 = (f32[128]{0:T(128)S(1)}, f32[128]{0:T(128)S(1)}) all-reduce(f32[128]{0:T(128)S(1)} %get-tuple-element.15, f32[128]{0:T(128)S(1)} %get-tuple-element.17), channel_id=1, replica_groups=mesh['img'=16,'proto'=16] {'proto'}, use_global_device_ids=true, to_apply=%region_3.0 | all-reduce | flops 256 | bytes 2048 | tf_op jit(solution)/shard_map/pmax | solution.py:19
  155.5 4.1 fusion.2
  159.7 26.4 %all-reduce = (f32[128]{0:T(128)S(1)}, f32[128]{0:T(128)S(1)}, f32[128]{0:T(128)S(1)}) all-reduce(f32[128]{0:T(128)S(1)} %get-tuple-element.5, f32[128]{0:T(128)S(1)} %get-tuple-element.4, f32[128]{0:T(128)S(1)} %get-tuple-element.3), channel_id=1, replica_groups=mesh['img'=16,'proto'=16] {'proto'}, use_global_device_ids=true, to_apply=%region_13.14 | all-reduce | flops 384 | bytes 3072 | tf_op jit(solution)/shard_map/psum | solution.py:24
  186.0 4.4 multiply_convert_fusion
  190.4 0.0 copy-start.1
  190.4 1.1 copy-done.1
  191.6 0.0 copy-start.2
  191.6 1.8 fusion.26
  193.4 0.0 all-reduce.6.cloned.1.call-update
  193.4 0.0 reduce-scatter.5.cloned.1.call-start
  193.5 106.0 %all-reduce.6.cloned.1.call-done = f32[128,256]{1,0:T(8,128)} async-done(((f32[128,256]{1,0:T(8,128)}), f32[128,256]{1,0:T(8,128)}) %all-reduce.6.cloned.1.call-update) | async-done | bytes 131088 | tf_op jit(solution)/shard_map/psum | solution.py:110
  299.5 0.0 copy-done.2
  299.5 1.0 multiply_reduce_fusion.1
  300.5 1.9 fusion.11
  302.4 0.0 reduce-scatter.5.cloned.1.call-update
  302.4 0.0 reduce-scatter.3.cloned.1.call-start
  302.5 5.1 %fusion.22 = f32[256,6144]{1,0:T(8,128)} fusion(bf16[128,6144]{1,0:T(8,128)(2,1)} %copy-done.1, f32[128,256]{1,0:T(8,128)S(1)} %copy-done.2, f32[128]{0:T(128)S(1)} %get-tuple-element.14), kind=kOutput, calls=%fused_computation.37 | convolution fusion | flops 402718720 | bytes 7995904 | tf_op jit(solution)/shard_map/dot_general | solution.py:42
  307.6 0.0 reduce-scatter.3.cloned.1.call-update
  307.6 0.6 multiply_reduce_fusion.4
  308.2 71.0 %reduce-scatter.5.cloned.1.call-done = f32[256,16]{0,1:T(8,128)} async-done(((f32[256,256]{0,1:T(8,128)}), f32[256,16]{0,1:T(8,128)}) %reduce-scatter.5.cloned.1.call-update) | async-done | bytes 16400 | tf_op jit(solution)/shard_map/reduce_scatter | solution.py:121
  379.3 91.2 %reduce-scatter.3.cloned.1.call-done = f32[16,6144]{1,0:T(8,128)} async-done(((f32[256,6144]{1,0:T(8,128)}), f32[16,6144]{1,0:T(8,128)}) %reduce-scatter.3.cloned.1.call-update) | async-done | bytes 393232 | tf_op jit(solution)/shard_map/reduce_scatter | solution.py:41
  (3 shorter events, 0.0 us)
Async XLA Ops:
  7.2 119.0 %copy-start = (bf16[256,6144]{1,0:T(8,128)(2,1)S(1)}, bf16[256,6144]{1,0:T(8,128)(2,1)}, u32[]{:S(2)}) copy-start(bf16[256,6144]{1,0:T(8,128)(2,1)} %param.15) | copy-start | bytes 9437188
  7.2 117.9 %all-reduce.8.cloned.1.call-start = ((), (), s32[]{:S(2)}) async-start(), calls=%async_computation.5 | async-start | bytes 524288 | tf_op jit(solution)/shard_map/psum | solution.py:85
  12.2 287.2 %all-reduce.6.cloned.1.call-start = ((), (), s32[]{:S(2)}) async-start(), calls=%async_computation.3 | async-start | bytes 262144 | tf_op jit(solution)/shard_map/psum | solution.py:110
  126.1 3.4 copy-start.3
  126.2 3.4 copy-start.4
  126.2 3.4 copy-start.5
  190.4 1.1 copy-start.1
  191.6 107.9 %copy-start.2 = (f32[128,256]{1,0:T(8,128)S(1)}, f32[128,256]{1,0:T(8,128)}, u32[]{:S(2)}) copy-start(f32[128,256]{1,0:T(8,128)} %get-tuple-element.10) | copy-start | bytes 393220
  193.4 185.8 %reduce-scatter.5.cloned.1.call-start = ((), (), s32[]{:S(2)}) async-start(), calls=%async_computation.4 | async-start | bytes 278528 | tf_op jit(solution)/shard_map/reduce_scatter | solution.py:121
  302.4 168.0 %reduce-scatter.3.cloned.1.call-start = ((), (), s32[]{:S(2)}) async-start(), calls=%async_computation.2 | async-start | bytes 6684672 | tf_op jit(solution)/shard_map/reduce_scatter | solution.py:41
Sparse Core Ops, SparseCore 0:
  12.3 112.6 all-reduce.7
  193.5 105.8 all-reduce.5
  303.5 75.7 reduce-scatter.4
  383.9 86.4 reduce-scatter.2
where the time goes:
time: 477 us
  waiting for transfers between devices  380 us (80%)
  blocking collectives  49.9 us (10%)
  matrix products  19.7 us (4%)
  between operations  14.6 us (3%)
  other arithmetic  11.2 us (2%)
    psum x1, waiting for transfers between devices, per_device(): lax.psum((partial_student, partial_teacher), 'proto')  112 us
    psum x1, waiting for transfers between devices, per_device(): grad_rows = lax.psum(partial_rows, 'proto')  106 us
    reduce_scatter x1, waiting for transfers between devices, prototype_gradient(): lax.psum_scatter(lax.dot_general(row_units, logit_gradient, (((0,), (0,))...  91.2 us
    reduce_scatter x1, waiting for transfers between devices, per_device(): lax.psum_scatter(local_term, 'img', scatter_dimension=1, tiled=True)  71 us
    psum x1, blocking collectives, scores(): lax.psum((jnp.sum(exp_student, axis=1), jnp.sum(exp_teacher, axis=1), jnp...  26.4 us
    pmax x1, blocking collectives, scores(): lax.pmax((jnp.max(logits_student, axis=1), jnp.max(logits_teacher, axis=1...  23.5 us
  transfers between devices with their start and end apart: 4, of which 4 were waited for; matrix products, arithmetic and copies ran while one was open for 1% of the time, Pallas kernels for 0%

commit v1 on v0

v1 whole, which is shorter than its diff:
```python
import functools

import jax
import jax.numpy as jnp
from jax import lax
from jax.experimental import pallas as pl
from jax.experimental.pallas import tpu as pltpu
from jax.sharding import PartitionSpec as P

EPSILON = 1e-06
STUDENT_SCALE = 10.0
TEACHER_SCALE = 25.0
GRAD_SCALE = 40960.0
MESH = pl.DeviceIdType.MESH
F32 = jnp.float32
BF16 = jnp.bfloat16

SIDE = 4
IMG = 16
ROWS = 128
BOT = 256
TILE = 512


def wait_bytes(ref, sem):
    pltpu.make_async_copy(ref, ref, sem).wait()


def kernel(
    tok_s_h,
    tok_t_h,
    cnt_ref,
    idx_h,
    bs_h,
    bt_h,
    ps_h,
    pt_h,
    cen_h,
    loss_ref,
    gp_ref,
    gb_ref,
    tok_s,
    tok_t,
    idx,
    bs,
    bt,
    ps,
    pt,
    cen,
    ps_own,
    pt_own,
    rows_s,
    a1_src,
    a1_recv,
    a2_src,
    a2_recv,
    hid,
    b_buf,
    units,
    ls_buf,
    lt_buf,
    st_buf,
    tot_buf,
    d_src,
    d_recv,
    e_buf,
    ps_own_t,
    pt_own_t,
    cen_own_t,
    g_acc,
    g_src,
    g_recv,
    f_src,
    f_recv,
    load_sem,
    a1_sem,
    a2_sem,
    b_sem,
    c_sem,
    t_sem,
    d_sem,
    e_sem,
    f_sem,
    g_sem,
    ag_send,
    ag_recv,
    sh_send,
    sh_recv,
):
    i = lax.axis_index("img")
    p = lax.axis_index("proto")
    x, y = i // SIDE, i % SIDE
    z, c = p // 2, p % 2
    width = ps_own.shape[1]
    tiles = ps.shape[1] // TILE

    barrier = pltpu.get_barrier_semaphore()

    def greet(k, carry):
        pl.semaphore_signal(barrier, inc=1, device_id=(i, (p + k) % 16), device_id_type=MESH)
        pl.semaphore_signal(barrier, inc=1, device_id=((i + k) % IMG, p), device_id_type=MESH)
        return carry

    lax.fori_loop(1, 16, greet, 0)

    own_columns = pl.ds(pl.multiple_of(i * width, 128), width)
    loads = [
        pltpu.make_async_copy(src, dst, load_sem.at[n])
        for n, (src, dst) in enumerate(
            (
                (idx_h, idx),
                (tok_s_h.at[0], tok_s),
                (bs_h, bs),
                (tok_t_h.at[0], tok_t),
                (bt_h, bt),
                (cen_h, cen),
                (ps_h.at[:, own_columns], ps_own),
                (pt_h.at[:, own_columns], pt_own),
                (ps_h, ps),
                (pt_h, pt),
            )
        )
    ]
    for load in loads:
        load.start()

    loads[0].wait()
    spread = jnp.broadcast_to(idx[...].astype(F32), (ROWS, ROWS)).T
    patch = lax.broadcasted_iota(jnp.int32, (ROWS, ROWS), 1).astype(F32)
    picker = jnp.concatenate(
        [(spread == patch).astype(F32), (spread == patch + 128.0).astype(F32)], axis=1
    ).astype(BF16)
    loads[1].wait()
    rows_s[...] = jnp.dot(picker, tok_s[...], preferred_element_type=F32).astype(BF16)
    loads[2].wait()
    part_s = jnp.dot(rows_s[...], bs[...], preferred_element_type=F32)
    loads[3].wait()
    rows_t = jnp.dot(picker, tok_t[...], preferred_element_type=F32).astype(BF16)
    loads[4].wait()
    part_t = jnp.dot(rows_t, bt[...], preferred_element_type=F32)
    a1_src[...] = jnp.where(c == 0, part_t, part_s)
    a2_src[...] = jnp.where(c == 0, part_s, part_t).reshape(8, 16, BOT)

    pl.semaphore_wait(barrier, 30)

    sibling = p + 1 - 2 * c
    a1 = pltpu.make_async_remote_copy(
        a1_src, a1_recv, a1_sem.at[0], a1_sem.at[1], device_id=(i, sibling), device_id_type=MESH
    )
    a1.start()
    loads[5].wait()
    loads[6].wait()
    ps_own_t[...] = ps_own[...].astype(F32).T.astype(BF16)
    loads[7].wait()
    pt_own_t[...] = pt_own[...].astype(F32).T.astype(BF16)
    for q in range(width // 128):
        cen_own_t[pl.ds(128 * q, 128), :] = jnp.broadcast_to(
            cen[pl.ds(i * (width // 128) + q, 1), :], (128, 128)
        ).T
    a1.wait_recv()
    a2_src[...] = a2_src[...] + a1_recv[...].reshape(8, 16, BOT)

    def a2_send(k, carry):
        z2 = (z + k) % 8
        pltpu.make_async_remote_copy(
            a2_src.at[z2],
            a2_recv.at[k - 1],
            a2_sem.at[0],
            a2_sem.at[1],
            device_id=(i, z2 * 2 + c),
            device_id_type=MESH,
        ).start()
        return carry

    lax.fori_loop(1, 8, a2_send, 0)
    wait_bytes(a2_recv, a2_sem.at[1])
    total = a2_src[z]
    for k in range(7):
        total = total + a2_recv[k]
    inv = lax.rsqrt(jnp.sum(total * total, axis=1, keepdims=True) + EPSILON)
    hid[0] = total
    hid[1] = jnp.broadcast_to(inv, (16, BOT))
    b_buf[p] = (total * inv).astype(BF16)

    def b_send(k, carry):
        pltpu.make_async_remote_copy(
            b_buf.at[p],
            b_buf.at[p],
            b_sem.at[0],
            b_sem.at[1],
            device_id=(i, (p + k) % 16),
            device_id_type=MESH,
        ).start()
        return carry

    lax.fori_loop(1, 16, b_send, 0)
    loads[8].wait()
    loads[9].wait()
    wait_bytes(b_buf.at[pl.ds(0, 15)], b_sem.at[1])
    units[0, 0, 0] = jnp.concatenate([b_buf[2 * k] for k in range(8)], axis=0)
    units[1, 0, 0] = jnp.concatenate([b_buf[2 * k + 1] for k in range(8)], axis=0)

    def neighbour(along_x, step):
        if along_x:
            return ((x + step) % SIDE) * SIDE + y
        return x * SIDE + (y + step) % SIDE

    def gather_copy(half, stage, forward):
        first = stage < 2
        along_x = (half == 0) == first
        step = 1 if forward else SIDE - 1
        base = 64 * half
        if stage % 2 == 0:
            src_slot, dst_slot, rows = 0, (3 if forward else 1), pl.ds(base, 64)
        else:
            src_slot, dst_slot = (3 if forward else 1), 2
            rows = pl.ds(base if forward else base + 32, 32)
        line = 0 if first else slice(None)

        def view(slot):
            if along_x:
                return units.at[c, slot, 0, rows] if first else units.at[c, slot, :, rows]
            return units.at[c, 0, slot, rows] if first else units.at[c, :, slot, rows]

        n = half * 8 + stage * 2 + (0 if forward else 1)
        return pltpu.make_async_remote_copy(
            view(src_slot),
            view(dst_slot),
            ag_send.at[n],
            ag_recv.at[n],
            device_id=(neighbour(along_x, step), p),
            device_id_type=MESH,
        )

    gather = [
        [[gather_copy(half, stage, forward) for forward in (True, False)] for stage in range(4)]
        for half in range(2)
    ]

    def gather_start(stage):
        for half in range(2):
            for copy in gather[half][stage]:
                copy.start()

    def gather_wait(stage):
        for half in range(2):
            for copy in gather[half][stage]:
                copy.wait_recv()

    def share_copy(half, second):
        rows = pl.ds(64 * half, 64)
        if half == 0:
            ref = units.at[c, :, pl.ds(1, 3), rows] if second else units.at[c, pl.ds(1, 3), 0, rows]
        else:
            ref = units.at[c, pl.ds(1, 3), :, rows] if second else units.at[c, 0, pl.ds(1, 3), rows]
        n = half * 2 + second
        return ref, pltpu.make_async_remote_copy(
            ref, ref, sh_send.at[n], sh_recv.at[n], device_id=(i, sibling), device_id_type=MESH
        )

    share = [[share_copy(half, second) for second in range(2)] for half in range(2)]

    gather_start(0)

    def logits(j, carry):
        top_s, top_t = carry
        columns = pl.ds(pl.multiple_of(j * TILE, TILE), TILE)
        logit_s = jnp.dot(units[0, 0, 0], ps[:, columns], preferred_element_type=F32) * STUDENT_SCALE
        ls_buf[:, columns] = logit_s
        raw_t = jnp.dot(units[1, 0, 0], pt[:, columns], preferred_element_type=F32)
        for q in range(TILE // 128):
            lanes = slice(128 * q, 128 * (q + 1))
            center = cen[pl.ds(j * (TILE // 128) + q, 1), :]
            logit_t = (raw_t[:, lanes] - center) * TEACHER_SCALE
            lt_buf[:, pl.ds(pl.multiple_of(j * TILE + 128 * q, 128), 128)] = logit_t
            top_s = jnp.maximum(top_s, logit_s[:, lanes])
            top_t = jnp.maximum(top_t, logit_t)
        return top_s, top_t

    low = jnp.full((ROWS, 128), -jnp.inf, F32)
    tops = lax.fori_loop(0, tiles, logits, (low, low))
    top_s = jnp.max(tops[0], axis=1, keepdims=True)
    top_t = jnp.max(tops[1], axis=1, keepdims=True)
    gather_wait(0)
    gather_start(1)

    def sums(j, carry):
        sum_s, sum_t, cross = carry
        for q in range(TILE // 128):
            columns = pl.ds(pl.multiple_of(j * TILE + 128 * q, 128), 128)
            logit_s = ls_buf[:, columns]
            exp_s = jnp.exp(logit_s - top_s)
            exp_t = jnp.exp(lt_buf[:, columns] - top_t)
            ls_buf[:, columns] = exp_s
            lt_buf[:, columns] = exp_t
            sum_s = sum_s + exp_s
            sum_t = sum_t + exp_t
            cross = cross + exp_t * logit_s
        return sum_s, sum_t, cross

    zero = jnp.zeros((ROWS, 128), F32)
    sum_s, sum_t, cross = lax.fori_loop(0, tiles, sums, (zero, zero, zero))
    lane = lax.broadcasted_iota(jnp.int32, (ROWS, 128), 1)
    table = jnp.where(lane == 0, top_s, jnp.where(lane == 1, top_t, 0.0))
    for n, value in ((2, sum_s), (3, sum_t), (4, cross)):
        table = jnp.where(lane == n, jnp.sum(value, axis=1, keepdims=True), table)
    st_buf[p] = table.T[:8]

    def c_send(k, carry):
        pltpu.make_async_remote_copy(
            st_buf.at[p],
            st_buf.at[p],
            c_sem.at[0],
            c_sem.at[1],
            device_id=(i, (p + k) % 16),
            device_id_type=MESH,
        ).start()
        return carry

    lax.fori_loop(1, 16, c_send, 0)
    gather_wait(1)
    gather_start(2)
    share[0][0][1].start()
    share[1][0][1].start()
    wait_bytes(st_buf.at[pl.ds(0, 15)], c_sem.at[1])
    all_top_s, all_top_t = st_buf[:, 0, :], st_buf[:, 1, :]
    max_s = jnp.max(all_top_s, axis=0, keepdims=True)
    max_t = jnp.max(all_top_t, axis=0, keepdims=True)
    scale_t = jnp.exp(all_top_t - max_t)
    total_s = jnp.sum(st_buf[:, 2, :] * jnp.exp(all_top_s - max_s), axis=0, keepdims=True)
    total_t = jnp.sum(st_buf[:, 3, :] * scale_t, axis=0, keepdims=True)
    total_x = jnp.sum(st_buf[:, 4, :] * scale_t, axis=0, keepdims=True)
    count = jnp.full((1, 128), cnt_ref[0], jnp.int32)
    live = lax.broadcasted_iota(jnp.int32, (1, 128), 1) < count
    weight = jnp.where(live, 1.0 / count.astype(F32), 0.0).astype(BF16).astype(F32)
    factor_s = GRAD_SCALE * weight / total_s
    factor_t = GRAD_SCALE * weight / total_t
    tot_buf[0] = jnp.concatenate(
        [max_s, factor_s, max_t, factor_t, jnp.zeros((4, 128), F32)], axis=0
    )

    def t_send(k, carry):
        dx, dy = k // SIDE, k % SIDE
        target = ((x + SIDE - dx) % SIDE) * SIDE + (y + SIDE - dy) % SIDE
        pltpu.make_async_remote_copy(
            tot_buf.at[0],
            tot_buf.at[k],
            t_sem.at[0],
            t_sem.at[1],
            device_id=(target, p),
            device_id_type=MESH,
        ).start()
        return carry

    lax.fori_loop(1, IMG, t_send, 0)
    loss_rows = -(total_x / total_t - max_s - jnp.log(total_s))
    loss_ref[0] = jnp.sum(weight * loss_rows)
    own = st_buf[p]
    near_s = factor_s * jnp.exp(own[0:1] - max_s)
    near_t = factor_t * jnp.exp(own[1:2] - max_t)
    near = jnp.concatenate([near_s, near_t, jnp.zeros((126, 128), F32)], axis=0).T
    near_s, near_t = near[:, 0:1], near[:, 1:2]

    def rows_gradient(j, carry):
        columns = pl.ds(pl.multiple_of(j * TILE, TILE), TILE)
        grad = (ls_buf[:, columns] * near_s - lt_buf[:, columns] * near_t).astype(BF16)
        return carry + lax.dot_general(
            grad, ps[:, columns], (((1,), (1,)), ((), ())), preferred_element_type=F32
        )

    d_src[...] = lax.fori_loop(0, tiles, rows_gradient, jnp.zeros((ROWS, BOT), F32)).reshape(
        8, 16, BOT
    )

    def d_send(k, carry):
        z2 = (z + k) % 8
        pltpu.make_async_remote_copy(
            d_src.at[z2],
            d_recv.at[p],
            d_sem.at[0],
            d_sem.at[1],
            device_id=(i, z2 * 2),
            device_id_type=MESH,
        ).start()
        return carry

    lax.fori_loop(1, 8, d_send, 0)

    @pl.when(c == 1)
    def _():
        d_send(0, 0)

    gather_wait(2)
    gather_start(3)
    gather_wait(3)
    share[0][1][1].start()
    share[1][1][1].start()

    @pl.when(c == 0)
    def _():
        d_recv[p] = d_src[z]
        wait_bytes(d_recv.at[pl.ds(0, 15)], d_sem.at[1])
        grad = d_recv[0]
        for k in range(1, 16):
            grad = grad + d_recv[k]
        hidden, inverse = hid[0], hid[1]
        inner = jnp.sum(hidden * grad, axis=1, keepdims=True)
        e_buf[z] = (
            grad * inverse - hidden * inner * (inverse * inverse * inverse)
        ).astype(BF16)

        def e_send(k, carry):
            pltpu.make_async_remote_copy(
                e_buf.at[z],
                e_buf.at[z],
                e_sem.at[0],
                e_sem.at[1],
                device_id=(i, (p + k) % 16),
                device_id_type=MESH,
            ).start()
            return carry

        lax.fori_loop(1, 16, e_send, 0)

    for half in range(2):
        for second in range(2):
            other = share[half][second][1]
            other.wait_recv()
    wait_bytes(tot_buf.at[pl.ds(1, 15)], t_sem.at[1])
    g_acc[...] = jnp.zeros_like(g_acc)

    def protos_gradient(k, carry):
        dx, dy = k // 2, (k % 2) * 2
        unit_s = units[0, dx, pl.ds(dy, 2)].reshape(2 * ROWS, BOT)
        unit_t = units[1, dx, pl.ds(dy, 2)].reshape(2 * ROWS, BOT)
        both = tot_buf[pl.ds(2 * k, 2)]
        wide = jnp.concatenate([both[0], both[1]], axis=1)
        for q in range(width // 128):
            block = pl.ds(128 * q, 128)
            contract = (((1,), (1,)), ((), ()))
            logit_s = (
                lax.dot_general(ps_own_t[block, :], unit_s, contract, preferred_element_type=F32)
                * STUDENT_SCALE
            )
            raw_t = lax.dot_general(pt_own_t[block, :], unit_t, contract, preferred_element_type=F32)
            center = cen_own_t[block, 0:1]
            logit_t = (raw_t - center) * TEACHER_SCALE
            grad = (
                jnp.exp(logit_s - wide[0:1]) * wide[1:2] - jnp.exp(logit_t - wide[2:3]) * wide[3:4]
            ).astype(BF16)
            g_acc[block, :] += jnp.dot(grad, unit_s, preferred_element_type=F32)
        return carry

    lax.fori_loop(0, IMG // 2, protos_gradient, 0)
    g_src[...] = g_acc[...].T.astype(BF16).reshape(IMG, 16, width)
    g_recv[i] = g_src[i]

    def g_send(k, carry):
        target = (i + k) % IMG
        pltpu.make_async_remote_copy(
            g_src.at[target],
            g_recv.at[i],
            g_sem.at[0],
            g_sem.at[1],
            device_id=(target, p),
            device_id_type=MESH,
        ).start()
        return carry

    lax.fori_loop(1, IMG, g_send, 0)

    @pl.when(c == 0)
    def _():
        wait_bytes(e_buf.at[pl.ds(0, 7)], e_sem.at[1])

    @pl.when(c == 1)
    def _():
        wait_bytes(e_buf, e_sem.at[1])

    grad_hidden = e_buf[...].reshape(ROWS, BOT)
    f_src[...] = (
        lax.dot_general(
            grad_hidden, rows_s[...], (((0,), (0,)), ((), ())), preferred_element_type=F32
        )
    ).reshape(IMG, 16, BOT)

    def f_send(k, carry):
        target = (i + k) % IMG
        pltpu.make_async_remote_copy(
            f_src.at[target],
            f_recv.at[i],
            f_sem.at[0],
            f_sem.at[1],
            device_id=(target, p),
            device_id_type=MESH,
        ).start()
        return carry

    lax.fori_loop(1, IMG, f_send, 0)
    f_recv[i] = f_src[i]

    wait_bytes(g_recv.at[pl.ds(0, 15)], g_sem.at[1])
    for k in range(IMG):
        gp_ref[:, width * k : width * (k + 1)] = g_recv[k].astype(F32)
    wait_bytes(f_recv.at[pl.ds(0, 15)], f_sem.at[1])
    bottleneck = f_recv[0]
    for k in range(1, IMG):
        bottleneck = bottleneck + f_recv[k]
    gb_ref[...] = bottleneck.T

    a1.wait_send()
    wait_bytes(a2_recv, a2_sem.at[0])
    wait_bytes(b_buf.at[pl.ds(0, 15)], b_sem.at[0])
    wait_bytes(st_buf.at[pl.ds(0, 15)], c_sem.at[0])
    wait_bytes(tot_buf.at[pl.ds(0, 15)], t_sem.at[0])
    wait_bytes(g_recv.at[pl.ds(0, 15)], g_sem.at[0])
    wait_bytes(f_recv.at[pl.ds(0, 15)], f_sem.at[0])

    @pl.when(c == 0)
    def _():
        wait_bytes(d_src.at[pl.ds(0, 7)], d_sem.at[0])
        wait_bytes(b_buf.at[pl.ds(0, 15)], e_sem.at[0])

    @pl.when(c == 1)
    def _():
        wait_bytes(d_src, d_sem.at[0])

    for half in range(2):
        for stage in range(4):
            for copy in gather[half][stage]:
                copy.wait_send()
        for second in range(2):
            share[half][second][1].wait_send()


def per_device(
    student_patch_tokens,
    teacher_patch_tokens,
    mask_counts,
    mask_index,
    student_bottleneck,
    teacher_bottleneck,
    student_protos,
    teacher_protos,
    center,
):
    patches, features = student_patch_tokens.shape[1:]
    protos = student_protos.shape[1]
    width = protos // IMG
    anywhere = pl.BlockSpec(memory_space=pl.ANY)
    dma = pltpu.SemaphoreType.DMA
    outs = pl.pallas_call(
        kernel,
        out_shape=(
            jax.ShapeDtypeStruct((1,), F32),
            jax.ShapeDtypeStruct((BOT // IMG, protos), F32),
            jax.ShapeDtypeStruct((features, BOT // IMG), F32),
        ),
        in_specs=[
            anywhere,
            anywhere,
            pl.BlockSpec(memory_space=pltpu.SMEM),
            anywhere,
            anywhere,
            anywhere,
            anywhere,
            anywhere,
            anywhere,
        ],
        out_specs=(
            pl.BlockSpec(memory_space=pltpu.SMEM),
            pl.BlockSpec(memory_space=pltpu.VMEM),
            pl.BlockSpec(memory_space=pltpu.VMEM),
        ),
        scratch_shapes=[
            pltpu.VMEM((patches, features), BF16),
            pltpu.VMEM((patches, features), BF16),
            pltpu.VMEM((1, ROWS), jnp.int32),
            pltpu.VMEM((features, BOT), BF16),
            pltpu.VMEM((features, BOT), BF16),
            pltpu.VMEM((BOT, protos), BF16),
            pltpu.VMEM((BOT, protos), BF16),
            pltpu.VMEM((protos // 128, 128), F32),
            pltpu.VMEM((BOT, width), BF16),
            pltpu.VMEM((BOT, width), BF16),
            pltpu.VMEM((ROWS, features), BF16),
            pltpu.VMEM((ROWS, BOT), F32),
            pltpu.VMEM((ROWS, BOT), F32),
            pltpu.VMEM((8, 16, BOT), F32),
            pltpu.VMEM((7, 16, BOT), F32),
            pltpu.VMEM((2, 16, BOT), F32),
            pltpu.VMEM((16, 16, BOT), BF16),
            pltpu.VMEM((2, SIDE, SIDE, ROWS, BOT), BF16),
            pltpu.VMEM((ROWS, protos), F32),
            pltpu.VMEM((ROWS, protos), F32),
            pltpu.VMEM((16, 8, 128), F32),
            pltpu.VMEM((IMG, 8, 128), F32),
            pltpu.VMEM((8, 16, BOT), F32),
            pltpu.VMEM((16, 16, BOT), F32),
            pltpu.VMEM((8, 16, BOT), BF16),
            pltpu.VMEM((width, BOT), BF16),
            pltpu.VMEM((width, BOT), BF16),
            pltpu.VMEM((width, 128), F32),
            pltpu.VMEM((width, BOT), F32),
            pltpu.VMEM((IMG, 16, width), BF16),
            pltpu.VMEM((IMG, 16, width), BF16),
            pltpu.VMEM((IMG, 16, features), F32),
            pltpu.VMEM((IMG, 16, features), F32),
            dma((10,)),
            dma((2,)),
            dma((2,)),
            dma((2,)),
            dma((2,)),
            dma((2,)),
            dma((2,)),
            dma((2,)),
            dma((2,)),
            dma((2,)),
            dma((16,)),
            dma((16,)),
            dma((4,)),
            dma((4,)),
        ],
        compiler_params=pltpu.CompilerParams(
            collective_id=0, has_side_effects=True, vmem_limit_bytes=56 * 1024 * 1024
        ),
    )(
        student_patch_tokens,
        teacher_patch_tokens,
        mask_counts,
        mask_index,
        student_bottleneck,
        teacher_bottleneck,
        student_protos,
        teacher_protos,
        center.reshape(protos // 128, 128),
    )
    return outs


def solution(mesh):
    placed = (
        P("img", None, "proto"),
        P("img", None, "proto"),
        P("img"),
        P("img", None),
        P("proto", None),
        P("proto", None),
        P(None, "proto"),
        P(None, "proto"),
        P("proto"),
    )
    return jax.shard_map(
        per_device,
        mesh=mesh,
        in_specs=placed,
        out_specs=(P("img"), P("img", "proto"), P("proto", "img")),
        check_vma=False,
    )
```

time: 477 us -> 67.2 us (0.14)
  waiting for transfers between devices: 380 us -> 0 us
  Pallas kernels: 0 us -> 60.7 us
  blocking collectives: 49.9 us -> 0 us
  matrix products: 19.7 us -> 0 us
  between operations: 14.6 us -> 2.99 us
  other arithmetic: 11.2 us -> 0 us
    psum x2 -> x0, waiting for transfers between devices: 218 us -> none  [the longest x1 112 us: per_device(): lax.psum((partial_student, partial_teacher), 'proto')]
    reduce_scatter x2 -> x0, waiting for transfers between devices: 162 us -> none  [the longest x1 91.2 us: prototype_gradient(): lax.psum_scatter(lax.dot_general(row_units, logit_gradient, (((0,), (0,))...]
    pallas_call x0 -> x1, Pallas kernels: none -> 60.7 us  [per_device(): pl.pallas_call(kernel, out_shape=(jax.ShapeDtypeStruct((1,), F32), jax.Sh...]
    psum x1 -> x0, blocking collectives: 26.4 us -> none  [scores(): lax.psum((jnp.sum(exp_student, axis=1), jnp.sum(exp_teacher, axis=1), jnp...]
    pmax x1 -> x0, blocking collectives: 23.5 us -> none  [scores(): lax.pmax((jnp.max(logits_student, axis=1), jnp.max(logits_teacher, axis=1...]
    dot_general x8 -> x0, matrix products: 19.7 us -> none  [the longest x1 5.14 us: prototype_gradient(): lax.dot_general(row_units, logit_gradient, (((0,), (0,)), ((), ())), pref...]
    reduce_sum x4 -> x0, other arithmetic: 6.8 us -> none  [the longest x1 4.1 us: scores(): jnp.sum(exp_teacher, axis=1)]
  transfers between devices with their start and end apart: 4 -> 0, of which waited for: 4 -> 0; matrix products, arithmetic and copies ran while one was open for 1% -> 0% of each run, Pallas kernels for 0% -> 0%
where the time goes in v1:
time: 67.2 us; the launch traced here: 67 us
  Pallas kernels  60.7 us (90%)
  local copies, waits for them, and re-layouts  3.35 us (5%)
  between operations  2.99 us (4%)
    pallas_call x1, Pallas kernels, per_device(): pl.pallas_call(kernel, out_shape=(jax.ShapeDtypeStruct((1,), F32), jax.Sh...  60.7 us
    unnamed x1, local copies, waits for them, and re-layouts  1.77 us
    pallas_call x1, local copies, waits for them, and re-layouts, per_device(): pl.pallas_call(kernel, out_shape=(jax.ShapeDtypeStruct((1,), F32), jax.Sh...  1.58 us

profile of v1, /device:TPU:1, one launch (start us, length us, event | category | flops | bytes accessed | tf_op | source)
XLA Modules:
  0.0 67.0 jit_solution(11024053368644588598)
XLA Ops:
  1.3 60.7 %shard_map.112 = (f32[1]{0:T(128)}, f32[16,6144]{1,0:T(8,128)}, f32[256,16]{1,0:T(8,128)}) custom-call(bf16[1,256,256]{2,1,0:T(8,128)(2,1)} %tok_s_h.1, bf16[1,256,256]{2,1,0:T(8,128)(2,1)} %tok_t_h.1, s32[1]{0:T(128)S(6)} %copy.15.cnt_ref, s32[1,128]{1,0:T(1,128)} %idx_h.1, bf16[256,256]{1,0:T(8,128)(2,1)} %bs_h.1, bf16[256,256]{1,0:T(8,128)(2,1)} %bt_h.1, ...), custom_call_target="tpu_custom_call" | custom-call | tf_op jit(solution)/shard_map/pallas_call | solution.py:552
  62.0 1.6 %copy.12 = f32[256,16]{0,1:T(8,128)} copy(f32[256,16]{1,0:T(8,128)} %get-tuple-element.5) | data formatting | bytes 32768 | tf_op jit(solution)/shard_map/pallas_call | solution.py:552
  64.1 1.8 %copy.17 = f32[16,6144]{1,0:T(8,128)} copy(f32[16,6144]{1,0:T(8,128)} %get-tuple-element.10) | data formatting | bytes 786432

commit v2 on v1

v2 whole, which is shorter than its diff:
```python
import math

import jax
import jax.numpy as jnp
from jax import lax
from jax.experimental import pallas as pl
from jax.experimental.pallas import tpu as pltpu
from jax.sharding import PartitionSpec as P

EPSILON = 1e-06
STUDENT_SCALE = 10.0
LOG2E = 1.0 / math.log(2.0)
STUDENT_2 = 10.0 * LOG2E
TEACHER_2 = 25.0 * LOG2E
GRAD_SCALE = 40960.0
MESH = pl.DeviceIdType.MESH
F32 = jnp.float32
BF16 = jnp.bfloat16

SIDE = 4
IMG = 16
DEEP = 8
ROWS = 128
BOT = 256
TILE = 1024
CONTRACT_LAST = (((1,), (1,)), ((), ()))
CONTRACT_FIRST = (((0,), (0,)), ((), ()))

Z_STEPS = (4, 3, 5, 2, 6, 1, 7)
PLANE_STEPS = tuple(
    sorted(
        ((dx, dy) for dx in range(SIDE) for dy in range(SIDE) if dx or dy),
        key=lambda d: -(min(d[0], SIDE - d[0]) + min(d[1], SIDE - d[1])),
    )
)


def wait_bytes(ref, sem):
    pltpu.make_async_copy(ref, ref, sem).wait()


def columns_of(rows):
    pad = jnp.zeros((128 - rows.shape[0], 128), F32)
    return jnp.concatenate([rows, pad], axis=0).T


def kernel(
    tok_s_h,
    tok_t_h,
    cnt_h,
    idx_h,
    bs_h,
    bt_h,
    ps_h,
    pt_h,
    cen_h,
    gp_h,
    gb_ref,
    loss_ref,
    tok_s,
    tok_t,
    cnt,
    idx,
    bs,
    bt,
    ps,
    pt,
    cen,
    ps_own,
    pt_own,
    rows_s,
    a1_src,
    a1_recv,
    a2_src,
    a2_recv,
    hid,
    b_buf,
    units,
    ls_buf,
    lt_buf,
    p_src,
    p_recv,
    ps_st,
    st_buf,
    tot_buf,
    d_src,
    d_recv,
    d_col,
    h_buf,
    e_buf,
    ps_own_t,
    pt_own_t,
    cen_own_t,
    g_acc,
    g_src,
    f_src,
    f_recv,
    load_sem,
    a1_sem,
    a2_sem,
    hid_sem,
    b_sem,
    b2_sem,
    p_sem,
    pst_sem,
    c_sem,
    t_sem,
    d_sem,
    h_sem,
    e_sem,
    f_sem,
    g_sem,
    ag_send,
    ag_recv,
    sh_send,
    sh_recv,
):
    i = lax.axis_index("img")
    p = lax.axis_index("proto")
    x, y = i // SIDE, i % SIDE
    z, c = p // 2, p % 2
    width = ps_own.shape[1]
    tiles = ps.shape[1] // TILE
    sibling = p + 1 - 2 * c
    core_0 = c == 0

    def z_peer(step):
        return (i, ((z + step) % DEEP) * 2 + c)

    def plane_peer(dx, dy):
        return ((x + dx) % SIDE) * SIDE + (y + dy) % SIDE

    def remote(src, dst, sems, device):
        return pltpu.make_async_remote_copy(
            src, dst, sems.at[0], sems.at[1], device_id=device, device_id_type=MESH
        )

    barrier = pltpu.get_barrier_semaphore()
    pl.semaphore_signal(barrier, inc=1, device_id=(i, sibling), device_id_type=MESH)
    for step in Z_STEPS:
        pl.semaphore_signal(barrier, inc=1, device_id=z_peer(step), device_id_type=MESH)
    for dx, dy in PLANE_STEPS:
        pl.semaphore_signal(barrier, inc=1, device_id=(plane_peer(dx, dy), p), device_id_type=MESH)

    own_columns = pl.ds(pl.multiple_of(i * width, 128), width)
    loads = [
        pltpu.make_async_copy(src, dst, load_sem.at[n])
        for n, (src, dst) in enumerate(
            (
                (idx_h, idx),
                (tok_s_h.at[0], tok_s),
                (bs_h, bs),
                (tok_t_h.at[0], tok_t),
                (bt_h, bt),
                (cen_h, cen),
                (ps_h.at[:, own_columns], ps_own),
                (pt_h.at[:, own_columns], pt_own),
                (ps_h, ps),
                (pt_h, pt),
                (cnt_h, cnt),
            )
        )
    ]
    for load in loads[:5]:
        load.start()

    loads[0].wait()
    spread = jnp.broadcast_to(idx[...].astype(F32), (ROWS, ROWS)).T
    patch = lax.broadcasted_iota(jnp.int32, (ROWS, ROWS), 1).astype(F32)
    picker = jnp.concatenate(
        [(spread == patch).astype(F32), (spread == patch + 128.0).astype(F32)], axis=1
    ).astype(BF16)
    loads[1].wait()
    rows_s[...] = jnp.dot(picker, tok_s[...], preferred_element_type=F32).astype(BF16)
    loads[3].wait()
    rows_t = jnp.dot(picker, tok_t[...], preferred_element_type=F32).astype(BF16)
    loads[2].wait()
    part_s = jnp.dot(rows_s[...], bs[...], preferred_element_type=F32)
    loads[4].wait()
    part_t = jnp.dot(rows_t, bt[...], preferred_element_type=F32)
    a1_src[...] = jnp.where(core_0, part_t, part_s).reshape(DEEP, 16, BOT)
    a2_src[...] = jnp.where(core_0, part_s, part_t).reshape(DEEP, 16, BOT)

    pl.semaphore_wait(barrier, 1 + len(Z_STEPS) + len(PLANE_STEPS))

    a1 = remote(a1_src, a1_recv, a1_sem, (i, sibling))
    a1.start()
    for load in loads[5:]:
        load.start()
    a1.wait_recv()
    a2_src[...] = a2_src[...] + a1_recv[...]
    for step in Z_STEPS:
        remote(
            a2_src.at[(z + step) % DEEP], a2_recv.at[step - 1], a2_sem, z_peer(step)
        ).start()

    for load in loads[5:8]:
        load.wait()
    ps_own_t[...] = ps_own[...].astype(F32).T.astype(BF16)
    pt_own_t[...] = pt_own[...].astype(F32).T.astype(BF16)
    for q in range(width // 128):
        cen_own_t[pl.ds(128 * q, 128), :] = jnp.broadcast_to(
            cen[pl.ds(i * (width // 128) + q, 1), :], (128, 128)
        ).T

    wait_bytes(a2_recv, a2_sem.at[1])
    total = a2_src[z]
    for k in range(DEEP - 1):
        total = total + a2_recv[k]
    inv = lax.rsqrt(jnp.sum(total * total, axis=1, keepdims=True) + EPSILON)
    b_buf[c, z] = (total * inv).astype(BF16)

    for step in Z_STEPS:
        remote(b_buf.at[c, z], b_buf.at[c, z], b_sem, z_peer(step)).start()
    hid[c] = total
    hidden_copy = remote(hid.at[c], hid.at[c], hid_sem, (i, sibling))
    hidden_copy.start()
    for load in loads[8:]:
        load.wait()
    wait_bytes(b_buf.at[c, pl.ds(0, DEEP - 1)], b_sem.at[1])
    b2 = remote(b_buf.at[c], b_buf.at[c], b2_sem, (i, sibling))
    b2.start()
    b2.wait_recv()
    units[:, 0, 0] = b_buf[...].reshape(2, ROWS, BOT)

    def gather_copy(half, stage, forward):
        first = stage < 2
        along_x = (half == 0) == first
        step = 1 if forward else SIDE - 1
        base = 64 * half
        if stage % 2 == 0:
            src_slot, dst_slot, rows = 0, (3 if forward else 1), pl.ds(base, 64)
        else:
            src_slot, dst_slot = (3 if forward else 1), 2
            rows = pl.ds(base if forward else base + 32, 32)

        def view(slot):
            if along_x:
                return units.at[c, slot, 0, rows] if first else units.at[c, slot, :, rows]
            return units.at[c, 0, slot, rows] if first else units.at[c, :, slot, rows]

        n = half * 8 + stage * 2 + (0 if forward else 1)
        return pltpu.make_async_remote_copy(
            view(src_slot),
            view(dst_slot),
            ag_send.at[n],
            ag_recv.at[n],
            device_id=(plane_peer(step, 0) if along_x else plane_peer(0, step), p),
            device_id_type=MESH,
        )

    gather = [
        [[gather_copy(half, stage, forward) for forward in (True, False)] for stage in range(4)]
        for half in range(2)
    ]

    def gather_start(stage):
        for half in range(2):
            for copy in gather[half][stage]:
                copy.start()

    def gather_wait(stage):
        for half in range(2):
            for copy in gather[half][stage]:
                copy.wait_recv()

    def share_copy(half, second):
        rows = pl.ds(64 * half, 64)
        if half == 0:
            ref = units.at[c, :, pl.ds(1, 3), rows] if second else units.at[c, pl.ds(1, 3), 0, rows]
        else:
            ref = units.at[c, pl.ds(1, 3), :, rows] if second else units.at[c, 0, pl.ds(1, 3), rows]
        n = half * 2 + second
        return pltpu.make_async_remote_copy(
            ref, ref, sh_send.at[n], sh_recv.at[n], device_id=(i, sibling), device_id_type=MESH
        )

    share = [[share_copy(half, second) for second in range(2)] for half in range(2)]

    gather_start(0)

    def logits(j, carry):
        top_s, top_t = carry
        columns = pl.ds(pl.multiple_of(j * TILE, TILE), TILE)
        raw_s = jnp.dot(units[0, 0, 0], ps[:, columns], preferred_element_type=F32)
        raw_t = jnp.dot(units[1, 0, 0], pt[:, columns], preferred_element_type=F32)
        for q in range(TILE // 128):
            lanes = slice(128 * q, 128 * (q + 1))
            here = pl.ds(pl.multiple_of(j * TILE + 128 * q, 128), 128)
            ls_buf[:, here] = raw_s[:, lanes]
            moved = raw_t[:, lanes] - cen[pl.ds(j * (TILE // 128) + q, 1), :]
            lt_buf[:, here] = moved
            top_s = jnp.maximum(top_s, raw_s[:, lanes])
            top_t = jnp.maximum(top_t, moved)
        return top_s, top_t

    low = jnp.full((ROWS, 128), -jnp.inf, F32)
    tops = lax.fori_loop(0, tiles, logits, (low, low))
    top_s = jnp.max(tops[0], axis=1, keepdims=True)
    top_t = jnp.max(tops[1], axis=1, keepdims=True)
    gather_wait(0)
    gather_start(1)

    shift_s = top_s * STUDENT_2
    shift_t = top_t * TEACHER_2

    def sums(j, carry):
        sum_s, sum_t, cross, acc_s, acc_t = carry
        columns = pl.ds(pl.multiple_of(j * TILE, TILE), TILE)
        part_s, part_t = [], []
        for q in range(TILE // 128):
            here = pl.ds(pl.multiple_of(j * TILE + 128 * q, 128), 128)
            raw_s = ls_buf[:, here]
            exp_s = jnp.exp2(raw_s * STUDENT_2 - shift_s)
            exp_t = jnp.exp2(lt_buf[:, here] * TEACHER_2 - shift_t)
            sum_s = sum_s + exp_s
            sum_t = sum_t + exp_t
            cross = cross + exp_t * raw_s
            part_s.append(exp_s.astype(BF16))
            part_t.append(exp_t.astype(BF16))
        acc_s = acc_s + lax.dot_general(
            jnp.concatenate(part_s, axis=1), ps[:, columns], CONTRACT_LAST, preferred_element_type=F32
        )
        acc_t = acc_t + lax.dot_general(
            jnp.concatenate(part_t, axis=1), ps[:, columns], CONTRACT_LAST, preferred_element_type=F32
        )
        return sum_s, sum_t, cross, acc_s, acc_t

    zero = jnp.zeros((ROWS, 128), F32)
    wide = jnp.zeros((ROWS, BOT), F32)
    sum_s, sum_t, cross, acc_s, acc_t = lax.fori_loop(
        0, tiles, sums, (zero, zero, zero, wide, wide)
    )
    p_src[...] = jnp.where(core_0, acc_t, acc_s)
    pair = remote(p_src, p_recv, p_sem, (i, sibling))
    pair.start()
    lane = lax.broadcasted_iota(jnp.int32, (ROWS, 128), 1)
    table = jnp.where(lane == 0, top_s, jnp.where(lane == 1, top_t, 0.0))
    for n, value in ((2, sum_s), (3, sum_t), (4, cross)):
        table = jnp.where(lane == n, jnp.sum(value, axis=1, keepdims=True), table)
    mine = table.T[:8]
    ps_st[0] = mine
    pair_stats = remote(ps_st.at[0], ps_st.at[1], pst_sem, (i, sibling))
    pair_stats.start()

    pair_stats.wait_recv()
    other = ps_st[1]
    best = jnp.maximum(mine[0:2], other[0:2])
    base = jnp.concatenate(
        [jnp.full((1, 128), STUDENT_2, F32), jnp.full((1, 128), TEACHER_2, F32)], axis=0
    )
    scale_mine = jnp.exp2((mine[0:2] - best) * base)
    scale_other = jnp.exp2((other[0:2] - best) * base)
    st_buf[z] = jnp.concatenate(
        [
            best,
            mine[2:4] * scale_mine + other[2:4] * scale_other,
            mine[4:5] * scale_mine[1:2] + other[4:5] * scale_other[1:2],
            jnp.zeros((3, 128), F32),
        ],
        axis=0,
    )
    for step in Z_STEPS:
        remote(st_buf.at[z], st_buf.at[z], c_sem, z_peer(step)).start()
    own_scale = columns_of(
        jnp.where(
            core_0,
            jnp.concatenate([scale_mine[0:1], scale_other[0:1]], axis=0),
            jnp.concatenate([scale_mine[1:2], scale_other[1:2]], axis=0),
        )
    )

    kept = jnp.where(core_0, acc_s, acc_t) * own_scale[:, 0:1]
    pair.wait_recv()
    d_src[...] = (kept + p_recv[...] * own_scale[:, 1:2]).reshape(DEEP, 16, BOT)
    for step in Z_STEPS:
        remote(d_src.at[(z + step) % DEEP], d_recv.at[z], d_sem, z_peer(step)).start()
    d_recv[z] = d_src[z]
    loads_count = jnp.full((1, 128), cnt[0], jnp.int32)
    live = lax.broadcasted_iota(jnp.int32, (1, 128), 1) < loads_count
    weight = jnp.where(live, 1.0 / loads_count.astype(F32), 0.0).astype(BF16).astype(F32)

    gather_wait(1)
    gather_start(2)
    share[0][0].start()
    share[1][0].start()

    wait_bytes(st_buf.at[pl.ds(0, DEEP - 1)], c_sem.at[1])
    all_top_s, all_top_t = st_buf[:, 0, :], st_buf[:, 1, :]
    max_s = jnp.max(all_top_s, axis=0, keepdims=True)
    max_t = jnp.max(all_top_t, axis=0, keepdims=True)
    scale_s = jnp.exp2((all_top_s - max_s) * STUDENT_2)
    scale_t = jnp.exp2((all_top_t - max_t) * TEACHER_2)
    total_s = jnp.sum(st_buf[:, 2, :] * scale_s, axis=0, keepdims=True)
    total_t = jnp.sum(st_buf[:, 3, :] * scale_t, axis=0, keepdims=True)
    total_x = jnp.sum(st_buf[:, 4, :] * scale_t, axis=0, keepdims=True)
    factor_s = GRAD_SCALE * weight / total_s
    factor_t = GRAD_SCALE * weight / total_t
    tot_buf[0] = jnp.concatenate(
        [max_s * STUDENT_2, factor_s, max_t * TEACHER_2, factor_t, jnp.zeros((4, 128), F32)], axis=0
    )

    for dx, dy in PLANE_STEPS:
        slot = ((SIDE - dx) % SIDE) * SIDE + (SIDE - dy) % SIDE
        remote(tot_buf.at[0], tot_buf.at[slot], t_sem, (plane_peer(dx, dy), p)).start()
    d_col[...] = columns_of(jnp.where(core_0, scale_s * factor_s, scale_t * factor_t))
    loss_rows = -(
        STUDENT_SCALE * (total_x / total_t) - STUDENT_SCALE * max_s - jnp.log(total_s)
    )
    loss_ref[...] = weight * loss_rows

    wait_bytes(d_recv.at[pl.ds(0, DEEP - 1)], d_sem.at[1])
    scales = d_col[pl.ds(pl.multiple_of(16 * z, 16), 16), :]
    half_grad = d_recv[0] * scales[:, 0:1]
    for k in range(1, DEEP):
        half_grad = half_grad + d_recv[k] * scales[:, k : k + 1]
    h_buf[c] = half_grad
    h_copy = remote(h_buf.at[c], h_buf.at[c], h_sem, (i, sibling))
    h_copy.start()

    gather_wait(2)
    gather_start(3)

    hidden_copy.wait_recv()
    hidden = hid[0]
    inverse = lax.rsqrt(jnp.sum(hidden * hidden, axis=1, keepdims=True) + EPSILON)
    h_copy.wait_recv()
    grad = h_buf[0] - h_buf[1]
    inner = jnp.sum(hidden * grad, axis=1, keepdims=True)
    e_buf[z] = (grad * inverse - hidden * inner * (inverse * inverse * inverse)).astype(BF16)
    for step in Z_STEPS:
        remote(e_buf.at[z], e_buf.at[z], e_sem, z_peer(step)).start()

    gather_wait(3)
    share[0][1].start()
    share[1][1].start()

    for half in range(2):
        for second in range(2):
            share[half][second].wait_recv()
    wait_bytes(tot_buf.at[pl.ds(1, IMG - 1)], t_sem.at[1])
    g_acc[...] = jnp.zeros_like(g_acc)

    def protos_gradient(k, carry):
        dx, dy = k // 2, (k % 2) * 2
        unit_s = units[0, dx, pl.ds(dy, 2)].reshape(2 * ROWS, BOT)
        unit_t = units[1, dx, pl.ds(dy, 2)].reshape(2 * ROWS, BOT)
        both = tot_buf[pl.ds(2 * k, 2)]
        along = jnp.concatenate([both[0], both[1]], axis=1)
        for q in range(width // 128):
            block = pl.ds(128 * q, 128)
            raw_s = lax.dot_general(
                ps_own_t[block, :], unit_s, CONTRACT_LAST, preferred_element_type=F32
            )
            raw_t = lax.dot_general(
                pt_own_t[block, :], unit_t, CONTRACT_LAST, preferred_element_type=F32
            )
            exp_s = jnp.exp2(raw_s * STUDENT_2 - along[0:1])
            exp_t = jnp.exp2((raw_t - cen_own_t[block, 0:1]) * TEACHER_2 - along[2:3])
            slope = (exp_s * along[1:2] - exp_t * along[3:4]).astype(BF16)
            g_acc[block, :] += jnp.dot(slope, unit_s, preferred_element_type=F32)
        return carry

    lax.fori_loop(0, IMG // 2, protos_gradient, 0)
    g_src[...] = g_acc[...].T.astype(BF16).reshape(IMG, 16, width)
    for dx, dy in PLANE_STEPS:
        target = plane_peer(dx, dy)
        remote(g_src.at[target], gp_h.at[:, own_columns], g_sem, (target, p)).start()
    keep = pltpu.make_async_copy(g_src.at[i], gp_h.at[:, own_columns], load_sem.at[0])
    keep.start()

    wait_bytes(e_buf.at[pl.ds(0, DEEP - 1)], e_sem.at[1])
    grad_hidden = e_buf[...].reshape(ROWS, BOT)
    f_src[...] = (
        lax.dot_general(grad_hidden, rows_s[...], CONTRACT_FIRST, preferred_element_type=F32)
        .astype(BF16)
        .reshape(IMG, 16, BOT)
    )
    for dx, dy in PLANE_STEPS:
        target = plane_peer(dx, dy)
        remote(f_src.at[target], f_recv.at[i], f_sem, (target, p)).start()
    f_recv[i] = f_src[i]

    a1.wait_send()
    wait_bytes(a2_recv, a2_sem.at[0])
    hidden_copy.wait_send()
    wait_bytes(b_buf.at[c, pl.ds(0, DEEP - 1)], b_sem.at[0])
    b2.wait_send()
    pair.wait_send()
    pair_stats.wait_send()
    wait_bytes(st_buf.at[pl.ds(0, DEEP - 1)], c_sem.at[0])
    wait_bytes(d_recv.at[pl.ds(0, DEEP - 1)], d_sem.at[0])
    wait_bytes(tot_buf.at[pl.ds(1, IMG - 1)], t_sem.at[0])
    h_copy.wait_send()
    wait_bytes(e_buf.at[pl.ds(0, DEEP - 1)], e_sem.at[0])
    for half in range(2):
        for stage in range(4):
            for copy in gather[half][stage]:
                copy.wait_send()
        for second in range(2):
            share[half][second].wait_send()
    wait_bytes(g_src.at[pl.ds(0, IMG - 1)], g_sem.at[0])
    wait_bytes(f_src.at[pl.ds(0, IMG - 1)], f_sem.at[0])
    keep.wait()

    wait_bytes(f_recv.at[pl.ds(0, IMG - 1)], f_sem.at[1])
    bottleneck = f_recv[0].astype(F32)
    for k in range(1, IMG):
        bottleneck = bottleneck + f_recv[k].astype(F32)
    gb_ref[...] = bottleneck
    wait_bytes(gp_h.at[:, pl.ds(0, (IMG - 1) * width)], g_sem.at[1])


def finish(gp_in, gb_in, loss_in, loss_ref, gp_ref, gb_ref):
    gp_ref[...] = gp_in[...].astype(F32)
    gb_ref[...] = gb_in[...]
    loss_ref[0] = jnp.sum(loss_in[...])


def per_device(
    student_patch_tokens,
    teacher_patch_tokens,
    mask_counts,
    mask_index,
    student_bottleneck,
    teacher_bottleneck,
    student_protos,
    teacher_protos,
    center,
):
    patches, features = student_patch_tokens.shape[1:]
    protos = student_protos.shape[1]
    width = protos // IMG
    in_hbm = pl.BlockSpec(memory_space=pltpu.HBM)
    in_vmem = pl.BlockSpec(memory_space=pltpu.VMEM)
    dma = pltpu.SemaphoreType.DMA
    parts = pl.pallas_call(
        kernel,
        out_shape=(
            jax.ShapeDtypeStruct((BOT // IMG, protos), BF16),
            jax.ShapeDtypeStruct((BOT // IMG, features), F32),
            jax.ShapeDtypeStruct((1, 128), F32),
        ),
        in_specs=[in_hbm] * 9,
        out_specs=(in_hbm, in_vmem, in_vmem),
        scratch_shapes=[
            pltpu.VMEM((patches, features), BF16),
            pltpu.VMEM((patches, features), BF16),
            pltpu.SMEM((1,), jnp.int32),
            pltpu.VMEM((1, ROWS), jnp.int32),
            pltpu.VMEM((features, BOT), BF16),
            pltpu.VMEM((features, BOT), BF16),
            pltpu.VMEM((BOT, protos), BF16),
            pltpu.VMEM((BOT, protos), BF16),
            pltpu.VMEM((protos // 128, 128), F32),
            pltpu.VMEM((BOT, width), BF16),
            pltpu.VMEM((BOT, width), BF16),
            pltpu.VMEM((ROWS, features), BF16),
            pltpu.VMEM((DEEP, 16, BOT), F32),
            pltpu.VMEM((DEEP, 16, BOT), F32),
            pltpu.VMEM((DEEP, 16, BOT), F32),
            pltpu.VMEM((DEEP - 1, 16, BOT), F32),
            pltpu.VMEM((2, 16, BOT), F32),
            pltpu.VMEM((2, DEEP, 16, BOT), BF16),
            pltpu.VMEM((2, SIDE, SIDE, ROWS, BOT), BF16),
            pltpu.VMEM((ROWS, protos), F32),
            pltpu.VMEM((ROWS, protos), F32),
            pltpu.VMEM((ROWS, BOT), F32),
            pltpu.VMEM((ROWS, BOT), F32),
            pltpu.VMEM((2, 8, 128), F32),
            pltpu.VMEM((DEEP, 8, 128), F32),
            pltpu.VMEM((IMG, 8, 128), F32),
            pltpu.VMEM((DEEP, 16, BOT), F32),
            pltpu.VMEM((DEEP, 16, BOT), F32),
            pltpu.VMEM((ROWS, 128), F32),
            pltpu.VMEM((2, 16, BOT), F32),
            pltpu.VMEM((DEEP, 16, BOT), BF16),
            pltpu.VMEM((width, BOT), BF16),
            pltpu.VMEM((width, BOT), BF16),
            pltpu.VMEM((width, 128), F32),
            pltpu.VMEM((width, BOT), F32),
            pltpu.VMEM((IMG, 16, width), BF16),
            pltpu.VMEM((IMG, 16, features), BF16),
            pltpu.VMEM((IMG, 16, features), BF16),
            dma((11,)),
        ]
        + [dma((2,))] * 14
        + [
            dma((16,)),
            dma((16,)),
            dma((4,)),
            dma((4,)),
        ],
        compiler_params=pltpu.CompilerParams(
            collective_id=0, has_side_effects=True, vmem_limit_bytes=56 * 1024 * 1024
        ),
    )(
        student_patch_tokens,
        teacher_patch_tokens,
        mask_counts,
        mask_index,
        student_bottleneck,
        teacher_bottleneck,
        student_protos,
        teacher_protos,
        center.reshape(protos // 128, 128),
    )
    image_loss, grad_protos, grad_bottleneck = pl.pallas_call(
        finish,
        out_shape=(
            jax.ShapeDtypeStruct((1,), F32),
            jax.ShapeDtypeStruct((BOT // IMG, protos), F32),
            jax.ShapeDtypeStruct((BOT // IMG, features), F32),
        ),
        in_specs=[in_vmem] * 3,
        out_specs=(pl.BlockSpec(memory_space=pltpu.SMEM), in_vmem, in_vmem),
    )(*parts)
    return image_loss, grad_protos, grad_bottleneck.T


def solution(mesh):
    placed = (
        P("img", None, "proto"),
        P("img", None, "proto"),
        P("img"),
        P("img", None),
        P("proto", None),
        P("proto", None),
        P(None, "proto"),
        P(None, "proto"),
        P("proto"),
    )
    return jax.shard_map(
        per_device,
        mesh=mesh,
        in_specs=placed,
        out_specs=(P("img"), P("img", "proto"), P("proto", "img")),
        check_vma=False,
    )
```

time: 67.2 us -> 60.2 us (0.90)
  local copies, waits for them, and re-layouts: 3.35 us -> 0 us
  Pallas kernels: 60.7 us -> 58.8 us
  between operations: 2.99 us -> 1.29 us
    pallas_call x1 -> x2, Pallas kernels: 60.7 us -> 58.8 us  [the longest x1 57.1 us: per_device(): pl.pallas_call(kernel, out_shape=(jax.ShapeDtypeStruct((BOT // IMG, proto...]
    unnamed x1 -> x0, local copies, waits for them, and re-layouts: 1.77 us -> none
    pallas_call x1 -> x0, local copies, waits for them, and re-layouts: 1.58 us -> none  [per_device(): pl.pallas_call(kernel, out_shape=(jax.ShapeDtypeStruct((1,), F32), jax.Sh...]
where the time goes in v2:
time: 60.2 us; the launch traced here: 60.1 us
  Pallas kernels  58.8 us (98%)
  between operations  1.29 us (2%)
    pallas_call x1, Pallas kernels, per_device(): pl.pallas_call(kernel, out_shape=(jax.ShapeDtypeStruct((BOT // IMG, proto...  57.1 us
    pallas_call x1, Pallas kernels, per_device(): pl.pallas_call(finish, out_shape=(jax.ShapeDtypeStruct((1,), F32), jax.Sh...  1.73 us

profile of v2, /device:TPU:1, one launch (start us, length us, event | category | flops | bytes accessed | tf_op | source)
XLA Modules:
  0.0 60.1 jit_solution(7399621158035897195)
XLA Ops:
  1.3 57.1 %shard_map.112 = (bf16[16,6144]{1,0:T(8,128)(2,1)}, f32[16,256]{1,0:T(8,128)}, f32[1,128]{1,0:T(1,128)}) custom-call(bf16[1,256,256]{2,1,0:T(8,128)(2,1)} %tok_s_h.1, bf16[1,256,256]{2,1,0:T(8,128)(2,1)} %tok_t_h.1, s32[1]{0:T(128)S(6)} %copy.12.cnt_h, s32[1,128]{1,0:T(1,128)} %idx_h.1, bf16[256,256]{1,0:T(8,128)(2,1)} %bs_h.1, bf16[256,256]{1,0:T(8,128)(2,1)} %bt_h.1, ...), custom_call_target="tpu_custom_call" | custom-call | tf_op jit(solution)/shard_map/pallas_call | solution.py:537
  58.4 1.7 %shard_map.113 = (f32[1]{0:T(128)}, f32[16,6144]{1,0:T(8,128)}, f32[16,256]{1,0:T(8,128)}) custom-call(bf16[16,6144]{1,0:T(8,128)(2,1)} %get-tuple-element.9.gp_in, f32[16,256]{1,0:T(8,128)} %get-tuple-element.10.gb_in, f32[1,128]{1,0:T(1,128)} %get-tuple-element.11.loss_in), custom_call_target="tpu_custom_call" | custom-call | tf_op jit(solution)/shard_map/pallas_call | solution.py:608

commit v3 on v2

--- a/solution.py
+++ b/solution.py
@@ -185,8 +185,6 @@
 
     a1 = remote(a1_src, a1_recv, a1_sem, (i, sibling))
     a1.start()
-    for load in loads[5:]:
-        load.start()
     a1.wait_recv()
     a2_src[...] = a2_src[...] + a1_recv[...]
     for step in Z_STEPS:
@@ -194,6 +192,8 @@
             a2_src.at[(z + step) % DEEP], a2_recv.at[step - 1], a2_sem, z_peer(step)
         ).start()
 
+    for load in loads[5:]:
+        load.start()
     for load in loads[5:8]:
         load.wait()
     ps_own_t[...] = ps_own[...].astype(F32).T.astype(BF16)
@@ -264,18 +264,23 @@
             for copy in gather[half][stage]:
                 copy.wait_recv()
 
-    def share_copy(half, second):
+    def share_copy(half, part):
         rows = pl.ds(64 * half, 64)
-        if half == 0:
-            ref = units.at[c, :, pl.ds(1, 3), rows] if second else units.at[c, pl.ds(1, 3), 0, rows]
+        if part == 0:
+            ref = units.at[c, pl.ds(1, 3), 0, rows] if half == 0 else units.at[c, 0, pl.ds(1, 3), rows]
         else:
-            ref = units.at[c, pl.ds(1, 3), :, rows] if second else units.at[c, 0, pl.ds(1, 3), rows]
-        n = half * 2 + second
+            slot = (1, 3, 2)[part - 1]
+            ref = units.at[c, :, slot, rows] if half == 0 else units.at[c, slot, :, rows]
+        n = half * 4 + part
         return pltpu.make_async_remote_copy(
             ref, ref, sh_send.at[n], sh_recv.at[n], device_id=(i, sibling), device_id_type=MESH
         )
 
-    share = [[share_copy(half, second) for second in range(2)] for half in range(2)]
+    share = [[share_copy(half, part) for half in range(2)] for part in range(4)]
+
+    def share_start(part):
+        for copy in share[part]:
+            copy.start()
 
     gather_start(0)
 
@@ -298,8 +303,6 @@
     tops = lax.fori_loop(0, tiles, logits, (low, low))
     top_s = jnp.max(tops[0], axis=1, keepdims=True)
     top_t = jnp.max(tops[1], axis=1, keepdims=True)
-    gather_wait(0)
-    gather_start(1)
 
     shift_s = top_s * STUDENT_2
     shift_t = top_t * TEACHER_2
@@ -328,9 +331,10 @@
 
     zero = jnp.zeros((ROWS, 128), F32)
     wide = jnp.zeros((ROWS, BOT), F32)
-    sum_s, sum_t, cross, acc_s, acc_t = lax.fori_loop(
-        0, tiles, sums, (zero, zero, zero, wide, wide)
-    )
+    state = lax.fori_loop(0, tiles // 3, sums, (zero, zero, zero, wide, wide))
+    gather_wait(0)
+    gather_start(1)
+    sum_s, sum_t, cross, acc_s, acc_t = lax.fori_loop(tiles // 3, tiles, sums, state)
     p_src[...] = jnp.where(core_0, acc_t, acc_s)
     pair = remote(p_src, p_recv, p_sem, (i, sibling))
     pair.start()
@@ -342,6 +346,9 @@
     ps_st[0] = mine
     pair_stats = remote(ps_st.at[0], ps_st.at[1], pst_sem, (i, sibling))
     pair_stats.start()
+    gather_wait(1)
+    gather_start(2)
+    share_start(0)
 
     pair_stats.wait_recv()
     other = ps_st[1]
@@ -376,14 +383,14 @@
     for step in Z_STEPS:
         remote(d_src.at[(z + step) % DEEP], d_recv.at[z], d_sem, z_peer(step)).start()
     d_recv[z] = d_src[z]
-    loads_count = jnp.full((1, 128), cnt[0], jnp.int32)
-    live = lax.broadcasted_iota(jnp.int32, (1, 128), 1) < loads_count
-    weight = jnp.where(live, 1.0 / loads_count.astype(F32), 0.0).astype(BF16).astype(F32)
-
-    gather_wait(1)
-    gather_start(2)
-    share[0][0].start()
-    share[1][0].start()
+    count = jnp.full((1, 128), cnt[0, 0], jnp.int32)
+    live = lax.broadcasted_iota(jnp.int32, (1, 128), 1) < count
+    weight = jnp.where(live, 1.0 / count.astype(F32), 0.0).astype(BF16).astype(F32)
+
+    gather_wait(2)
+    gather_start(3)
+    share_start(1)
+    share_start(2)
 
     wait_bytes(st_buf.at[pl.ds(0, DEEP - 1)], c_sem.at[1])
     all_top_s, all_top_t = st_buf[:, 0, :], st_buf[:, 1, :]
@@ -418,8 +425,8 @@
     h_copy = remote(h_buf.at[c], h_buf.at[c], h_sem, (i, sibling))
     h_copy.start()
 
-    gather_wait(2)
-    gather_start(3)
+    gather_wait(3)
+    share_start(3)
 
     hidden_copy.wait_recv()
     hidden = hid[0]
@@ -431,37 +438,35 @@
     for step in Z_STEPS:
         remote(e_buf.at[z], e_buf.at[z], e_sem, z_peer(step)).start()
 
-    gather_wait(3)
-    share[0][1].start()
-    share[1][1].start()
-
-    for half in range(2):
-        for second in range(2):
-            share[half][second].wait_recv()
+    for part in share:
+        for copy in part:
+            copy.wait_recv()
     wait_bytes(tot_buf.at[pl.ds(1, IMG - 1)], t_sem.at[1])
     g_acc[...] = jnp.zeros_like(g_acc)
 
-    def protos_gradient(k, carry):
-        dx, dy = k // 2, (k % 2) * 2
-        unit_s = units[0, dx, pl.ds(dy, 2)].reshape(2 * ROWS, BOT)
-        unit_t = units[1, dx, pl.ds(dy, 2)].reshape(2 * ROWS, BOT)
-        both = tot_buf[pl.ds(2 * k, 2)]
-        along = jnp.concatenate([both[0], both[1]], axis=1)
+    def protos_gradient(dx, carry):
+        unit_s = units[0, dx].reshape(SIDE * ROWS, BOT)
+        unit_t = units[1, dx].reshape(SIDE * ROWS, BOT)
+        raw_s = lax.dot_general(ps_own_t[...], unit_s, CONTRACT_LAST, preferred_element_type=F32)
+        raw_t = lax.dot_general(pt_own_t[...], unit_t, CONTRACT_LAST, preferred_element_type=F32)
+        totals = tot_buf[pl.ds(SIDE * dx, SIDE)]
+        slopes = []
         for q in range(width // 128):
-            block = pl.ds(128 * q, 128)
-            raw_s = lax.dot_general(
-                ps_own_t[block, :], unit_s, CONTRACT_LAST, preferred_element_type=F32
-            )
-            raw_t = lax.dot_general(
-                pt_own_t[block, :], unit_t, CONTRACT_LAST, preferred_element_type=F32
-            )
-            exp_s = jnp.exp2(raw_s * STUDENT_2 - along[0:1])
-            exp_t = jnp.exp2((raw_t - cen_own_t[block, 0:1]) * TEACHER_2 - along[2:3])
-            slope = (exp_s * along[1:2] - exp_t * along[3:4]).astype(BF16)
-            g_acc[block, :] += jnp.dot(slope, unit_s, preferred_element_type=F32)
+            block = slice(128 * q, 128 * (q + 1))
+            center = cen_own_t[block, :]
+            line = []
+            for dy in range(SIDE):
+                lanes = slice(128 * dy, 128 * (dy + 1))
+                exp_s = jnp.exp2(raw_s[block, lanes] * STUDENT_2 - totals[dy, 0:1])
+                exp_t = jnp.exp2((raw_t[block, lanes] - center) * TEACHER_2 - totals[dy, 2:3])
+                line.append((exp_s * totals[dy, 1:2] - exp_t * totals[dy, 3:4]).astype(BF16))
+            slopes.append(jnp.concatenate(line, axis=1))
+        g_acc[...] += jnp.dot(
+            jnp.concatenate(slopes, axis=0), unit_s, preferred_element_type=F32
+        )
         return carry
 
-    lax.fori_loop(0, IMG // 2, protos_gradient, 0)
+    lax.fori_loop(0, SIDE, protos_gradient, 0)
     g_src[...] = g_acc[...].T.astype(BF16).reshape(IMG, 16, width)
     for dx, dy in PLANE_STEPS:
         target = plane_peer(dx, dy)
@@ -497,8 +502,9 @@
         for stage in range(4):
             for copy in gather[half][stage]:
                 copy.wait_send()
-        for second in range(2):
-            share[half][second].wait_send()
+    for part in share:
+        for copy in part:
+            copy.wait_send()
     wait_bytes(g_src.at[pl.ds(0, IMG - 1)], g_sem.at[0])
     wait_bytes(f_src.at[pl.ds(0, IMG - 1)], f_sem.at[0])
     keep.wait()
@@ -546,7 +552,7 @@
         scratch_shapes=[
             pltpu.VMEM((patches, features), BF16),
             pltpu.VMEM((patches, features), BF16),
-            pltpu.SMEM((1,), jnp.int32),
+            pltpu.SMEM((1, 1), jnp.int32),
             pltpu.VMEM((1, ROWS), jnp.int32),
             pltpu.VMEM((features, BOT), BF16),
             pltpu.VMEM((features, BOT), BF16),
@@ -588,8 +594,8 @@
         + [
             dma((16,)),
             dma((16,)),
-            dma((4,)),
-            dma((4,)),
+            dma((8,)),
+            dma((8,)),
         ],
         compiler_params=pltpu.CompilerParams(
             collective_id=0, has_side_effects=True, vmem_limit_bytes=56 * 1024 * 1024
@@ -597,7 +603,7 @@
     )(
         student_patch_tokens,
         teacher_patch_tokens,
-        mask_counts,
+        mask_counts.reshape(1, 1),
         mask_index,
         student_bottleneck,
         teacher_bottleneck,

time: 60.2 us -> 53.4 us (0.89)
  Pallas kernels: 58.8 us -> 52 us
    pallas_call x1, Pallas kernels: 57.1 us -> 50.2 us  [per_device(): pl.pallas_call(kernel, out_shape=(jax.ShapeDtypeStruct((BOT // IMG, proto...]
where the time goes in v3:
time: 53.4 us; the launch traced here: 53.3 us
  Pallas kernels  52 us (97%)
  between operations  1.29 us (2%)
    pallas_call x1, Pallas kernels, per_device(): pl.pallas_call(kernel, out_shape=(jax.ShapeDtypeStruct((BOT // IMG, proto...  50.2 us
    pallas_call x1, Pallas kernels, per_device(): pl.pallas_call(finish, out_shape=(jax.ShapeDtypeStruct((1,), F32), jax.Sh...  1.73 us

profile of v3, /device:TPU:1, one launch (start us, length us, event | category | flops | bytes accessed | tf_op | source)
XLA Modules:
  0.0 53.3 jit_solution(2303412092204821513)
XLA Ops:
  1.3 50.2 %shard_map.112 = (bf16[16,6144]{1,0:T(8,128)(2,1)}, f32[16,256]{1,0:T(8,128)}, f32[1,128]{1,0:T(1,128)}) custom-call(bf16[1,256,256]{2,1,0:T(8,128)(2,1)} %tok_s_h.1, bf16[1,256,256]{2,1,0:T(8,128)(2,1)} %tok_t_h.1, s32[1,1]{1,0:T(1,128)} %bitcast.3.cnt_h, s32[1,128]{1,0:T(1,128)} %idx_h.1, bf16[256,256]{1,0:T(8,128)(2,1)} %bs_h.1, bf16[256,256]{1,0:T(8,128)(2,1)} %bt_h.1, ...), custom_call_target="tpu_custom_call" | custom-call | tf_op jit(solution)/shard_map/pallas_call | solution.py:543
  51.5 1.7 %shard_map.113 = (f32[1]{0:T(128)}, f32[16,6144]{1,0:T(8,128)}, f32[16,256]{1,0:T(8,128)}) custom-call(bf16[16,6144]{1,0:T(8,128)(2,1)} %get-tuple-element.9.gp_in, f32[16,256]{1,0:T(8,128)} %get-tuple-element.10.gb_in, f32[1,128]{1,0:T(1,128)} %get-tuple-element.11.loss_in), custom_call_target="tpu_custom_call" | custom-call | tf_op jit(solution)/shard_map/pallas_call | solution.py:614

commit v4 on v3

--- a/solution.py
+++ b/solution.py
@@ -63,8 +63,7 @@
     idx,
     bs,
     bt,
-    ps,
-    pt,
+    pro,
     cen,
     ps_own,
     pt_own,
@@ -76,11 +75,11 @@
     hid,
     b_buf,
     units,
-    ls_buf,
-    lt_buf,
+    raw,
     p_src,
     p_recv,
-    ps_st,
+    o_st,
+    c_st,
     st_buf,
     tot_buf,
     d_src,
@@ -102,7 +101,8 @@
     b_sem,
     b2_sem,
     p_sem,
-    pst_sem,
+    ost_sem,
+    cst_sem,
     c_sem,
     t_sem,
     d_sem,
@@ -120,9 +120,12 @@
     x, y = i // SIDE, i % SIDE
     z, c = p // 2, p % 2
     width = ps_own.shape[1]
-    tiles = ps.shape[1] // TILE
+    tiles = pro.shape[2] // TILE
     sibling = p + 1 - 2 * c
     core_0 = c == 0
+    o = 1 - c
+    base_c = jnp.where(core_0, STUDENT_2, TEACHER_2)
+    base_o = jnp.where(core_0, TEACHER_2, STUDENT_2)
 
     def z_peer(step):
         return (i, ((z + step) % DEEP) * 2 + c)
@@ -152,11 +155,11 @@
                 (bs_h, bs),
                 (tok_t_h.at[0], tok_t),
                 (bt_h, bt),
-                (cen_h, cen),
+                (cen_h, cen.at[1]),
                 (ps_h.at[:, own_columns], ps_own),
                 (pt_h.at[:, own_columns], pt_own),
-                (ps_h, ps),
-                (pt_h, pt),
+                (ps_h, pro.at[0]),
+                (pt_h, pro.at[1]),
                 (cnt_h, cnt),
             )
         )
@@ -192,6 +195,7 @@
             a2_src.at[(z + step) % DEEP], a2_recv.at[step - 1], a2_sem, z_peer(step)
         ).start()
 
+    cen[0] = jnp.zeros_like(cen[0])
     for load in loads[5:]:
         load.start()
     for load in loads[5:8]:
@@ -200,7 +204,7 @@
     pt_own_t[...] = pt_own[...].astype(F32).T.astype(BF16)
     for q in range(width // 128):
         cen_own_t[pl.ds(128 * q, 128), :] = jnp.broadcast_to(
-            cen[pl.ds(i * (width // 128) + q, 1), :], (128, 128)
+            cen[1, pl.ds(i * (width // 128) + q, 1), :], (128, 128)
         ).T
 
     wait_bytes(a2_recv, a2_sem.at[1])
@@ -220,8 +224,7 @@
     wait_bytes(b_buf.at[c, pl.ds(0, DEEP - 1)], b_sem.at[1])
     b2 = remote(b_buf.at[c], b_buf.at[c], b2_sem, (i, sibling))
     b2.start()
-    b2.wait_recv()
-    units[:, 0, 0] = b_buf[...].reshape(2, ROWS, BOT)
+    units[c, 0, 0] = b_buf[c].reshape(ROWS, BOT)
 
     def gather_copy(half, stage, forward):
         first = stage < 2
@@ -284,104 +287,105 @@
 
     gather_start(0)
 
-    def logits(j, carry):
-        top_s, top_t = carry
-        columns = pl.ds(pl.multiple_of(j * TILE, TILE), TILE)
-        raw_s = jnp.dot(units[0, 0, 0], ps[:, columns], preferred_element_type=F32)
-        raw_t = jnp.dot(units[1, 0, 0], pt[:, columns], preferred_element_type=F32)
-        for q in range(TILE // 128):
-            lanes = slice(128 * q, 128 * (q + 1))
-            here = pl.ds(pl.multiple_of(j * TILE + 128 * q, 128), 128)
-            ls_buf[:, here] = raw_s[:, lanes]
-            moved = raw_t[:, lanes] - cen[pl.ds(j * (TILE // 128) + q, 1), :]
-            lt_buf[:, here] = moved
-            top_s = jnp.maximum(top_s, raw_s[:, lanes])
-            top_t = jnp.maximum(top_t, moved)
-        return top_s, top_t
-
-    low = jnp.full((ROWS, 128), -jnp.inf, F32)
-    tops = lax.fori_loop(0, tiles, logits, (low, low))
-    top_s = jnp.max(tops[0], axis=1, keepdims=True)
-    top_t = jnp.max(tops[1], axis=1, keepdims=True)
-
-    shift_s = top_s * STUDENT_2
-    shift_t = top_t * TEACHER_2
-
-    def sums(j, carry):
-        sum_s, sum_t, cross, acc_s, acc_t = carry
-        columns = pl.ds(pl.multiple_of(j * TILE, TILE), TILE)
-        part_s, part_t = [], []
-        for q in range(TILE // 128):
-            here = pl.ds(pl.multiple_of(j * TILE + 128 * q, 128), 128)
-            raw_s = ls_buf[:, here]
-            exp_s = jnp.exp2(raw_s * STUDENT_2 - shift_s)
-            exp_t = jnp.exp2(lt_buf[:, here] * TEACHER_2 - shift_t)
-            sum_s = sum_s + exp_s
-            sum_t = sum_t + exp_t
-            cross = cross + exp_t * raw_s
-            part_s.append(exp_s.astype(BF16))
-            part_t.append(exp_t.astype(BF16))
-        acc_s = acc_s + lax.dot_general(
-            jnp.concatenate(part_s, axis=1), ps[:, columns], CONTRACT_LAST, preferred_element_type=F32
+    def logits(kind):
+        def step(j, top):
+            columns = pl.ds(pl.multiple_of(j * TILE, TILE), TILE)
+            product = jnp.dot(units[kind, 0, 0], pro[kind, :, columns], preferred_element_type=F32)
+            for q in range(TILE // 128):
+                moved = product[:, 128 * q : 128 * (q + 1)] - cen[
+                    kind, pl.ds(j * (TILE // 128) + q, 1), :
+                ]
+                raw[kind, :, pl.ds(pl.multiple_of(j * TILE + 128 * q, 128), 128)] = moved
+                top = jnp.maximum(top, moved)
+            return top
+
+        top = lax.fori_loop(0, tiles, step, jnp.full((ROWS, 128), -jnp.inf, F32), unroll=True)
+        return jnp.max(top, axis=1, keepdims=True)
+
+    top_c = logits(c)
+    b2.wait_recv()
+    units[o, 0, 0] = b_buf[o].reshape(ROWS, BOT)
+    top_o = logits(o)
+
+    def sums(kind, top, base):
+        shift = top * base
+
+        def step(j, carry):
+            total, cross, acc = carry
+            parts = []
+            for q in range(TILE // 128):
+                here = pl.ds(pl.multiple_of(j * TILE + 128 * q, 128), 128)
+                power = jnp.exp2(raw[kind, :, here] * base - shift)
+                total = total + power
+                cross = cross + power * raw[1 - kind, :, here]
+                parts.append(power.astype(BF16))
+            columns = pl.ds(pl.multiple_of(j * TILE, TILE), TILE)
+            acc = acc + lax.dot_general(
+                jnp.concatenate(parts, axis=1),
+                pro[0, :, columns],
+                CONTRACT_LAST,
+                preferred_element_type=F32,
+            )
+            return total, cross, acc
+
+        zero = jnp.zeros((ROWS, 128), F32)
+        total, cross, acc = lax.fori_loop(
+            0, tiles, step, (zero, zero, jnp.zeros((ROWS, BOT), F32)), unroll=True
         )
-        acc_t = acc_t + lax.dot_general(
-            jnp.concatenate(part_t, axis=1), ps[:, columns], CONTRACT_LAST, preferred_element_type=F32
-        )
-        return sum_s, sum_t, cross, acc_s, acc_t
-
-    zero = jnp.zeros((ROWS, 128), F32)
-    wide = jnp.zeros((ROWS, BOT), F32)
-    state = lax.fori_loop(0, tiles // 3, sums, (zero, zero, zero, wide, wide))
+        return total, cross, acc
+
+    def statistics(top, total, cross):
+        lane = lax.broadcasted_iota(jnp.int32, (ROWS, 128), 1)
+        table = jnp.where(lane == 0, top, 0.0)
+        for n, value in ((1, total), (2, cross)):
+            table = jnp.where(lane == n, jnp.sum(value, axis=1, keepdims=True), table)
+        return table.T[:8]
+
+    total_o, cross_o, acc_o = sums(o, top_o, base_o)
+    p_src[...] = acc_o
+    pair = remote(p_src, p_recv, p_sem, (i, sibling))
+    pair.start()
+    o_st[0] = statistics(top_o, total_o, cross_o)
+    pair_o = remote(o_st.at[0], o_st.at[1], ost_sem, (i, sibling))
+    pair_o.start()
     gather_wait(0)
     gather_start(1)
-    sum_s, sum_t, cross, acc_s, acc_t = lax.fori_loop(tiles // 3, tiles, sums, state)
-    p_src[...] = jnp.where(core_0, acc_t, acc_s)
-    pair = remote(p_src, p_recv, p_sem, (i, sibling))
-    pair.start()
-    lane = lax.broadcasted_iota(jnp.int32, (ROWS, 128), 1)
-    table = jnp.where(lane == 0, top_s, jnp.where(lane == 1, top_t, 0.0))
-    for n, value in ((2, sum_s), (3, sum_t), (4, cross)):
-        table = jnp.where(lane == n, jnp.sum(value, axis=1, keepdims=True), table)
-    mine = table.T[:8]
-    ps_st[0] = mine
-    pair_stats = remote(ps_st.at[0], ps_st.at[1], pst_sem, (i, sibling))
-    pair_stats.start()
+    total_c, cross_c, acc_c = sums(c, top_c, base_c)
+    c_st[0] = statistics(top_c, total_c, cross_c)
+    pair_c = remote(c_st.at[0], c_st.at[1], cst_sem, (i, sibling))
+    pair_c.start()
     gather_wait(1)
     gather_start(2)
     share_start(0)
 
-    pair_stats.wait_recv()
-    other = ps_st[1]
-    best = jnp.maximum(mine[0:2], other[0:2])
-    base = jnp.concatenate(
-        [jnp.full((1, 128), STUDENT_2, F32), jnp.full((1, 128), TEACHER_2, F32)], axis=0
-    )
-    scale_mine = jnp.exp2((mine[0:2] - best) * base)
-    scale_other = jnp.exp2((other[0:2] - best) * base)
+    def together(mine, theirs, base):
+        best = jnp.maximum(mine[0:1], theirs[0:1])
+        scale_mine = jnp.exp2((mine[0:1] - best) * base)
+        scale_theirs = jnp.exp2((theirs[0:1] - best) * base)
+        return best, mine[1:3] * scale_mine + theirs[1:3] * scale_theirs, scale_mine, scale_theirs
+
+    pair_o.wait_recv()
+    best_c, sums_c, scale_mine, scale_theirs = together(c_st[0], o_st[1], base_c)
+    own_scale = columns_of(jnp.concatenate([scale_mine, scale_theirs], axis=0))
+    pair.wait_recv()
+    d_src[...] = (acc_c * own_scale[:, 0:1] + p_recv[...] * own_scale[:, 1:2]).reshape(DEEP, 16, BOT)
+    for step in Z_STEPS:
+        remote(d_src.at[(z + step) % DEEP], d_recv.at[z], d_sem, z_peer(step)).start()
+
+    pair_c.wait_recv()
+    best_o, sums_o, _, _ = together(o_st[0], c_st[1], base_o)
     st_buf[z] = jnp.concatenate(
         [
-            best,
-            mine[2:4] * scale_mine + other[2:4] * scale_other,
-            mine[4:5] * scale_mine[1:2] + other[4:5] * scale_other[1:2],
+            jnp.where(core_0, best_c, best_o),
+            jnp.where(core_0, best_o, best_c),
+            jnp.where(core_0, sums_c[0:1], sums_o[0:1]),
+            jnp.where(core_0, sums_o, sums_c),
             jnp.zeros((3, 128), F32),
         ],
         axis=0,
     )
     for step in Z_STEPS:
         remote(st_buf.at[z], st_buf.at[z], c_sem, z_peer(step)).start()
-    own_scale = columns_of(
-        jnp.where(
-            core_0,
-            jnp.concatenate([scale_mine[0:1], scale_other[0:1]], axis=0),
-            jnp.concatenate([scale_mine[1:2], scale_other[1:2]], axis=0),
-        )
-    )
-
-    kept = jnp.where(core_0, acc_s, acc_t) * own_scale[:, 0:1]
-    pair.wait_recv()
-    d_src[...] = (kept + p_recv[...] * own_scale[:, 1:2]).reshape(DEEP, 16, BOT)
-    for step in Z_STEPS:
-        remote(d_src.at[(z + step) % DEEP], d_recv.at[z], d_sem, z_peer(step)).start()
     d_recv[z] = d_src[z]
     count = jnp.full((1, 128), cnt[0, 0], jnp.int32)
     live = lax.broadcasted_iota(jnp.int32, (1, 128), 1) < count
@@ -411,11 +415,6 @@
         slot = ((SIDE - dx) % SIDE) * SIDE + (SIDE - dy) % SIDE
         remote(tot_buf.at[0], tot_buf.at[slot], t_sem, (plane_peer(dx, dy), p)).start()
     d_col[...] = columns_of(jnp.where(core_0, scale_s * factor_s, scale_t * factor_t))
-    loss_rows = -(
-        STUDENT_SCALE * (total_x / total_t) - STUDENT_SCALE * max_s - jnp.log(total_s)
-    )
-    loss_ref[...] = weight * loss_rows
-
     wait_bytes(d_recv.at[pl.ds(0, DEEP - 1)], d_sem.at[1])
     scales = d_col[pl.ds(pl.multiple_of(16 * z, 16), 16), :]
     half_grad = d_recv[0] * scales[:, 0:1]
@@ -424,9 +423,6 @@
     h_buf[c] = half_grad
     h_copy = remote(h_buf.at[c], h_buf.at[c], h_sem, (i, sibling))
     h_copy.start()
-
-    gather_wait(3)
-    share_start(3)
 
     hidden_copy.wait_recv()
     hidden = hid[0]
@@ -437,6 +433,13 @@
     e_buf[z] = (grad * inverse - hidden * inner * (inverse * inverse * inverse)).astype(BF16)
     for step in Z_STEPS:
         remote(e_buf.at[z], e_buf.at[z], e_sem, z_peer(step)).start()
+
+    gather_wait(3)
+    share_start(3)
+    loss_rows = -(
+        STUDENT_SCALE * (total_x / total_t) - STUDENT_SCALE * max_s - jnp.log(total_s)
+    )
+    loss_ref[...] = weight * loss_rows
 
     for part in share:
         for copy in part:
@@ -492,7 +495,8 @@
     wait_bytes(b_buf.at[c, pl.ds(0, DEEP - 1)], b_sem.at[0])
     b2.wait_send()
     pair.wait_send()
-    pair_stats.wait_send()
+    pair_o.wait_send()
+    pair_c.wait_send()
     wait_bytes(st_buf.at[pl.ds(0, DEEP - 1)], c_sem.at[0])
     wait_bytes(d_recv.at[pl.ds(0, DEEP - 1)], d_sem.at[0])
     wait_bytes(tot_buf.at[pl.ds(1, IMG - 1)], t_sem.at[0])
@@ -556,9 +560,8 @@
             pltpu.VMEM((1, ROWS), jnp.int32),
             pltpu.VMEM((features, BOT), BF16),
             pltpu.VMEM((features, BOT), BF16),
-            pltpu.VMEM((BOT, protos), BF16),
-            pltpu.VMEM((BOT, protos), BF16),
-            pltpu.VMEM((protos // 128, 128), F32),
+            pltpu.VMEM((2, BOT, protos), BF16),
+            pltpu.VMEM((2, protos // 128, 128), F32),
             pltpu.VMEM((BOT, width), BF16),
             pltpu.VMEM((BOT, width), BF16),
             pltpu.VMEM((ROWS, features), BF16),
@@ -569,10 +572,10 @@
             pltpu.VMEM((2, 16, BOT), F32),
             pltpu.VMEM((2, DEEP, 16, BOT), BF16),
             pltpu.VMEM((2, SIDE, SIDE, ROWS, BOT), BF16),
-            pltpu.VMEM((ROWS, protos), F32),
-            pltpu.VMEM((ROWS, protos), F32),
+            pltpu.VMEM((2, ROWS, protos), F32),
             pltpu.VMEM((ROWS, BOT), F32),
             pltpu.VMEM((ROWS, BOT), F32),
+            pltpu.VMEM((2, 8, 128), F32),
             pltpu.VMEM((2, 8, 128), F32),
             pltpu.VMEM((DEEP, 8, 128), F32),
             pltpu.VMEM((IMG, 8, 128), F32),
@@ -590,7 +593,7 @@
             pltpu.VMEM((IMG, 16, features), BF16),
             dma((11,)),
         ]
-        + [dma((2,))] * 14
+        + [dma((2,))] * 15
         + [
             dma((16,)),
             dma((16,)),

time: 53.4 us -> 51.8 us (0.970)
  Pallas kernels: 52 us -> 50.1 us
    pallas_call x1, Pallas kernels: 50.2 us -> 48.4 us  [per_device(): pl.pallas_call(kernel, out_shape=(jax.ShapeDtypeStruct((BOT // IMG, proto...]
where the time goes in v4:
time: 51.8 us; the launch traced here: 51.4 us
  Pallas kernels  50.1 us (97%)
  between operations  1.29 us (2%)
    pallas_call x1, Pallas kernels, per_device(): pl.pallas_call(kernel, out_shape=(jax.ShapeDtypeStruct((BOT // IMG, proto...  48.4 us
    pallas_call x1, Pallas kernels, per_device(): pl.pallas_call(finish, out_shape=(jax.ShapeDtypeStruct((1,), F32), jax.Sh...  1.73 us

profile of v4, /device:TPU:1, one launch (start us, length us, event | category | flops | bytes accessed | tf_op | source)
XLA Modules:
  0.0 51.4 jit_solution(8959655230677251023)
XLA Ops:
  1.3 48.4 %shard_map.112 = (bf16[16,6144]{1,0:T(8,128)(2,1)}, f32[16,256]{1,0:T(8,128)}, f32[1,128]{1,0:T(1,128)}) custom-call(bf16[1,256,256]{2,1,0:T(8,128)(2,1)} %tok_s_h.1, bf16[1,256,256]{2,1,0:T(8,128)(2,1)} %tok_t_h.1, s32[1,1]{1,0:T(1,128)} %bitcast.3.cnt_h, s32[1,128]{1,0:T(1,128)} %idx_h.1, bf16[256,256]{1,0:T(8,128)(2,1)} %bs_h.1, bf16[256,256]{1,0:T(8,128)(2,1)} %bt_h.1, ...), custom_call_target="tpu_custom_call" | custom-call | tf_op jit(solution)/shard_map/pallas_call | solution.py:547
  49.6 1.7 %shard_map.113 = (f32[1]{0:T(128)}, f32[16,6144]{1,0:T(8,128)}, f32[16,256]{1,0:T(8,128)}) custom-call(bf16[16,6144]{1,0:T(8,128)(2,1)} %get-tuple-element.9.gp_in, f32[16,256]{1,0:T(8,128)} %get-tuple-element.10.gb_in, f32[1,128]{1,0:T(1,128)} %get-tuple-element.11.loss_in), custom_call_target="tpu_custom_call" | custom-call | tf_op jit(solution)/shard_map/pallas_call | solution.py:617

commit v5 on v4

--- a/solution.py
+++ b/solution.py
@@ -55,8 +55,8 @@
     pt_h,
     cen_h,
     gp_h,
-    gb_ref,
-    loss_ref,
+    gb_h,
+    loss_h,
     tok_s,
     tok_t,
     cnt,
@@ -93,7 +93,7 @@
     g_acc,
     g_src,
     f_src,
-    f_recv,
+    loss,
     load_sem,
     a1_sem,
     a2_sem,
@@ -138,13 +138,6 @@
             src, dst, sems.at[0], sems.at[1], device_id=device, device_id_type=MESH
         )
 
-    barrier = pltpu.get_barrier_semaphore()
-    pl.semaphore_signal(barrier, inc=1, device_id=(i, sibling), device_id_type=MESH)
-    for step in Z_STEPS:
-        pl.semaphore_signal(barrier, inc=1, device_id=z_peer(step), device_id_type=MESH)
-    for dx, dy in PLANE_STEPS:
-        pl.semaphore_signal(barrier, inc=1, device_id=(plane_peer(dx, dy), p), device_id_type=MESH)
-
     own_columns = pl.ds(pl.multiple_of(i * width, 128), width)
     loads = [
         pltpu.make_async_copy(src, dst, load_sem.at[n])
@@ -167,6 +160,13 @@
     for load in loads[:5]:
         load.start()
 
+    barrier = pltpu.get_barrier_semaphore()
+    pl.semaphore_signal(barrier, inc=1, device_id=(i, sibling), device_id_type=MESH)
+    for step in Z_STEPS:
+        pl.semaphore_signal(barrier, inc=1, device_id=z_peer(step), device_id_type=MESH)
+    for dx, dy in PLANE_STEPS:
+        pl.semaphore_signal(barrier, inc=1, device_id=(plane_peer(dx, dy), p), device_id_type=MESH)
+
     loads[0].wait()
     spread = jnp.broadcast_to(idx[...].astype(F32), (ROWS, ROWS)).T
     patch = lax.broadcasted_iota(jnp.int32, (ROWS, ROWS), 1).astype(F32)
@@ -306,6 +306,8 @@
     b2.wait_recv()
     units[o, 0, 0] = b_buf[o].reshape(ROWS, BOT)
     top_o = logits(o)
+    gather_wait(0)
+    gather_start(1)
 
     def sums(kind, top, base):
         shift = top * base
@@ -348,15 +350,10 @@
     o_st[0] = statistics(top_o, total_o, cross_o)
     pair_o = remote(o_st.at[0], o_st.at[1], ost_sem, (i, sibling))
     pair_o.start()
-    gather_wait(0)
-    gather_start(1)
     total_c, cross_c, acc_c = sums(c, top_c, base_c)
     c_st[0] = statistics(top_c, total_c, cross_c)
     pair_c = remote(c_st.at[0], c_st.at[1], cst_sem, (i, sibling))
     pair_c.start()
-    gather_wait(1)
-    gather_start(2)
-    share_start(0)
 
     def together(mine, theirs, base):
         best = jnp.maximum(mine[0:1], theirs[0:1])
@@ -371,6 +368,10 @@
     d_src[...] = (acc_c * own_scale[:, 0:1] + p_recv[...] * own_scale[:, 1:2]).reshape(DEEP, 16, BOT)
     for step in Z_STEPS:
         remote(d_src.at[(z + step) % DEEP], d_recv.at[z], d_sem, z_peer(step)).start()
+
+    gather_wait(1)
+    gather_start(2)
+    share_start(0)
 
     pair_c.wait_recv()
     best_o, sums_o, _, _ = together(o_st[0], c_st[1], base_o)
@@ -439,7 +440,9 @@
     loss_rows = -(
         STUDENT_SCALE * (total_x / total_t) - STUDENT_SCALE * max_s - jnp.log(total_s)
     )
-    loss_ref[...] = weight * loss_rows
+    loss[...] = weight * loss_rows
+    keep_loss = pltpu.make_async_copy(loss, loss_h, load_sem.at[1])
+    keep_loss.start()
 
     for part in share:
         for copy in part:
@@ -469,7 +472,7 @@
         )
         return carry
 
-    lax.fori_loop(0, SIDE, protos_gradient, 0)
+    lax.fori_loop(0, SIDE, protos_gradient, 0, unroll=True)
     g_src[...] = g_acc[...].T.astype(BF16).reshape(IMG, 16, width)
     for dx, dy in PLANE_STEPS:
         target = plane_peer(dx, dy)
@@ -486,8 +489,9 @@
     )
     for dx, dy in PLANE_STEPS:
         target = plane_peer(dx, dy)
-        remote(f_src.at[target], f_recv.at[i], f_sem, (target, p)).start()
-    f_recv[i] = f_src[i]
+        remote(f_src.at[target], gb_h.at[i], f_sem, (target, p)).start()
+    keep_part = pltpu.make_async_copy(f_src.at[i], gb_h.at[i], load_sem.at[2])
+    keep_part.start()
 
     a1.wait_send()
     wait_bytes(a2_recv, a2_sem.at[0])
@@ -513,17 +517,18 @@
     wait_bytes(f_src.at[pl.ds(0, IMG - 1)], f_sem.at[0])
     keep.wait()
 
-    wait_bytes(f_recv.at[pl.ds(0, IMG - 1)], f_sem.at[1])
-    bottleneck = f_recv[0].astype(F32)
-    for k in range(1, IMG):
-        bottleneck = bottleneck + f_recv[k].astype(F32)
-    gb_ref[...] = bottleneck
+    keep_loss.wait()
+    keep_part.wait()
     wait_bytes(gp_h.at[:, pl.ds(0, (IMG - 1) * width)], g_sem.at[1])
+    wait_bytes(gb_h.at[pl.ds(0, IMG - 1)], f_sem.at[1])
 
 
 def finish(gp_in, gb_in, loss_in, loss_ref, gp_ref, gb_ref):
     gp_ref[...] = gp_in[...].astype(F32)
-    gb_ref[...] = gb_in[...]
+    total = gb_in[0].astype(F32)
+    for k in range(1, IMG):
+        total = total + gb_in[k].astype(F32)
+    gb_ref[...] = total
     loss_ref[0] = jnp.sum(loss_in[...])
 
 
@@ -548,11 +553,11 @@
         kernel,
         out_shape=(
             jax.ShapeDtypeStruct((BOT // IMG, protos), BF16),
-            jax.ShapeDtypeStruct((BOT // IMG, features), F32),
+            jax.ShapeDtypeStruct((IMG, BOT // IMG, features), BF16),
             jax.ShapeDtypeStruct((1, 128), F32),
         ),
         in_specs=[in_hbm] * 9,
-        out_specs=(in_hbm, in_vmem, in_vmem),
+        out_specs=(in_hbm, in_hbm, in_hbm),
         scratch_shapes=[
             pltpu.VMEM((patches, features), BF16),
             pltpu.VMEM((patches, features), BF16),
@@ -590,7 +595,7 @@
             pltpu.VMEM((width, BOT), F32),
             pltpu.VMEM((IMG, 16, width), BF16),
             pltpu.VMEM((IMG, 16, features), BF16),
-            pltpu.VMEM((IMG, 16, features), BF16),
+            pltpu.VMEM((1, 128), F32),
             dma((11,)),
         ]
         + [dma((2,))] * 15

time: 51.8 us -> 50.4 us (0.973)
  Pallas kernels: 50.1 us -> 48.8 us
    pallas_call x1, Pallas kernels: 48.4 us -> 47 us  [per_device(): pl.pallas_call(kernel, out_shape=(jax.ShapeDtypeStruct((BOT // IMG, proto...]
where the time goes in v5:
time: 50.4 us; the launch traced here: 50.1 us
  Pallas kernels  48.8 us (97%)
  between operations  1.29 us (3%)
    pallas_call x1, Pallas kernels, per_device(): pl.pallas_call(kernel, out_shape=(jax.ShapeDtypeStruct((BOT // IMG, proto...  47 us
    pallas_call x1, Pallas kernels, per_device(): pl.pallas_call(finish, out_shape=(jax.ShapeDtypeStruct((1,), F32), jax.Sh...  1.79 us

profile of v5, /device:TPU:1, one launch (start us, length us, event | category | flops | bytes accessed | tf_op | source)
XLA Modules:
  0.0 50.1 jit_solution(13573456111217736696)
XLA Ops:
  1.3 47.0 %shard_map.112 = (bf16[16,6144]{1,0:T(8,128)(2,1)}, bf16[16,16,256]{2,1,0:T(8,128)(2,1)}, f32[1,128]{1,0:T(1,128)}) custom-call(bf16[1,256,256]{2,1,0:T(8,128)(2,1)} %tok_s_h.1, bf16[1,256,256]{2,1,0:T(8,128)(2,1)} %tok_t_h.1, s32[1,1]{1,0:T(1,128)} %bitcast.3.cnt_h, s32[1,128]{1,0:T(1,128)} %idx_h.1, bf16[256,256]{1,0:T(8,128)(2,1)} %bs_h.1, ...), custom_call_target="tpu_custom_call" | custom-call | tf_op jit(solution)/shard_map/pallas_call | solution.py:552
  48.3 1.8 %shard_map.113 = (f32[1]{0:T(128)}, f32[16,6144]{1,0:T(8,128)}, f32[16,256]{1,0:T(8,128)}) custom-call(bf16[16,6144]{1,0:T(8,128)(2,1)} %get-tuple-element.9.gp_in, bf16[16,16,256]{2,1,0:T(8,128)(2,1)} %get-tuple-element.10.gb_in, f32[1,128]{1,0:T(1,128)} %get-tuple-element.11.loss_in), custom_call_target="tpu_custom_call" | custom-call | tf_op jit(solution)/shard_map/pallas_call | solution.py:622
